TPU v7x, 256 devices: a whole 4x4x8 slice. The times are simulated.
256 devices in a mesh: lat: 16 (over z, x_lo), lon: 16 (over x_hi, y, core).
Axes of the slice: x: 4 (x_hi: 2, x_lo: 2; x = x_hi * 2 + x_lo), y: 4, z: 8, core: 2. Of those that a mesh axis runs over, the one named last changes fastest.
Arguments:
- tokens: bfloat16 [4, 192, 192, 512], P(None, 'lat', 'lon'), may hold values from -6 to 6
- cotangent: bfloat16 [4, 96, 96, 1024], P(None, 'lat', 'lon'), may hold values from -6 to 6
- first_inward: bfloat16 [512, 1536], replicated, may hold values from -0.25 to 0.25
- first_outward: bfloat16 [512, 512], replicated, may hold values from -0.25 to 0.25
- merge_weight: bfloat16 [2048, 1024], P('lon'), may hold values from -0.125 to 0.125
- second_inward: bfloat16 [1024, 3072], replicated, may hold values from -0.1875 to 0.1875
- second_outward: bfloat16 [1024, 1024], replicated, may hold values from -0.1875 to 0.1875
Outputs:
- second_out: bfloat16 [4, 96, 96, 1024], P(None, 'lat', 'lon')
- token_grad: bfloat16 [4, 192, 192, 512], P(None, 'lat', 'lon')
All inputs are finite; a program needn't handle non-finite values.
Results may differ from a plain program's by a relative error of at most 0.023.
Values may be sent and summed in bfloat16 or wider, within the bound.
A program may use at most 128 MiB of HBM per device.

v0:
```python
import jax
import jax.numpy as jnp
from jax import lax
from jax.sharding import PartitionSpec as P

HEADS1 = 8
HEADS2 = 16


eps_norm = 1e-05


def from_behind(value, axis, steps):
    count = lax.axis_size(axis)
    pairs = [(source, (source + steps) % count) for source in range(count)]
    return lax.ppermute(value, axis, pairs)


def from_partner(array, axis, apart):
    return lax.ppermute(array, axis, [(i, i ^ 1 << apart) for i in range(lax.axis_size(axis))])


def normalize(vector):
    center = vector - jnp.mean(vector, axis=-1, keepdims=True)
    spread = jnp.mean(center * center, axis=-1, keepdims=True)
    return center * lax.rsqrt(spread + eps_norm)


def normalize_round(grid_field):
    return normalize(grid_field).astype(jnp.bfloat16)


def to_windows(grid_field, span):
    levels, lat_cells, lon_cells, channels = grid_field.shape
    shaped = grid_field.reshape(
        levels // 2, 2, lat_cells // 6, 6, lon_cells // span, span, channels
    )
    return shaped.transpose(0, 2, 4, 1, 3, 5, 6).reshape(-1, 12 * span, channels)


def from_windows(blocks, levels, lat_cells, lon_cells, span):
    channels = blocks.shape[-1]
    shaped = blocks.reshape(levels // 2, lat_cells // 6, lon_cells // span, 2, 6, span, channels)
    return shaped.transpose(0, 3, 1, 4, 2, 5, 6).reshape(levels, lat_cells, lon_cells, channels)


def region_labels(levels, lat_cells, offset, lat_total):
    level_part = (jnp.arange(levels, dtype=jnp.int32) >= levels - 1).astype(jnp.int32)
    row_part = (offset + jnp.arange(lat_cells, dtype=jnp.int32) >= lat_total - 3).astype(jnp.int32)
    return level_part[:, None] * 2 + row_part[None, :]


def window_labels(labels, lon_cells, span):
    spread_out = jnp.broadcast_to(labels[:, :, None, None], labels.shape + (lon_cells, 1))
    return to_windows(spread_out, span)[:, :, 0]


def attend(queries, keys_in, values_in, query_labels, key_labels, head_count):
    number, query_len, channels = queries.shape
    key_len = keys_in.shape[1]
    head_size = channels // head_count
    query_heads = queries.astype(jnp.float32).reshape(number, query_len, head_count, head_size)
    key_heads = keys_in.astype(jnp.float32).reshape(number, key_len, head_count, head_size)
    value_heads = values_in.astype(jnp.float32).reshape(number, key_len, head_count, head_size)
    scores = jnp.einsum("nqhd,nkhd->nhqk", query_heads, key_heads) * head_size ** (-0.5)
    allowed = query_labels[:, None, :, None] == key_labels[:, None, None, :]
    raised = jnp.where(allowed, jnp.exp(scores), 0.0)
    shares = (raised / jnp.sum(raised, axis=-1, keepdims=True)).astype(jnp.bfloat16)
    blended = jnp.einsum("nhqk,nkhd->nqhd", shares.astype(jnp.float32), value_heads)
    return blended.reshape(number, query_len, channels).astype(jnp.bfloat16)


def move_rows(grid_field, lat_step, lon_step, direction):
    grid_field = jnp.roll(grid_field, -direction, axis=0)
    lat_cells = grid_field.shape[1]
    begin_at = 0 if direction == 1 else lat_cells - lat_step
    arrived = from_behind(
        lax.slice_in_dim(grid_field, begin_at, begin_at + lat_step, axis=1), "lat", -direction
    )
    remain = (
        lax.slice_in_dim(grid_field, lat_step, lat_cells, axis=1)
        if direction == 1
        else lax.slice_in_dim(grid_field, 0, lat_cells - lat_step, axis=1)
    )
    grid_field = jnp.concatenate([remain, arrived] if direction == 1 else [arrived, remain], axis=1)
    lon_cells = grid_field.shape[2]
    begin_at = 0 if direction == 1 else lon_cells - lon_step
    arrived = from_behind(
        lax.slice_in_dim(grid_field, begin_at, begin_at + lon_step, axis=2), "lon", -direction
    )
    remain = (
        lax.slice_in_dim(grid_field, lon_step, lon_cells, axis=2)
        if direction == 1
        else lax.slice_in_dim(grid_field, 0, lon_cells - lon_step, axis=2)
    )
    return jnp.concatenate([remain, arrived] if direction == 1 else [arrived, remain], axis=2)


def local_section(grid_field, inward, outward, labels, head_count):
    levels, lat_cells, lon_cells, channels = grid_field.shape
    blocks = to_windows(grid_field, 12)
    number = blocks.shape[0]
    triple = jnp.dot(
        blocks.reshape(-1, channels), inward, preferred_element_type=jnp.float32
    ).astype(jnp.bfloat16)
    triple = triple.reshape(number, -1, 3 * channels)
    blended = attend(
        triple[..., :channels],
        triple[..., channels : 2 * channels],
        triple[..., 2 * channels :],
        labels,
        labels,
        head_count,
    )
    projected = jnp.dot(
        blended.reshape(-1, channels), outward, preferred_element_type=jnp.float32
    ).astype(jnp.bfloat16)
    return from_windows(projected.reshape(number, -1, channels), levels, lat_cells, lon_cells, 12)


def merge_patches(grid_field):
    levels, lat_cells, lon_cells, channels = grid_field.shape
    shaped = grid_field.reshape(levels, lat_cells // 2, 2, lon_cells // 2, 2, channels).transpose(
        0, 1, 3, 2, 4, 5
    )
    return shaped.reshape(levels, lat_cells // 2, lon_cells // 2, 4 * channels)


def local(
    tokens, cotangent, first_inward, first_outward, merge_weight, second_inward, second_outward
):
    levels, lat_cells, lon_cells, width_one = tokens.shape
    width_two = second_outward.shape[0]
    half_rows = lat_cells // 2
    half_cols = lon_cells // 2
    lat_index = lax.axis_index("lat")
    lat_devices = lax.axis_size("lat")
    wide_tokens = tokens.astype(jnp.float32)
    normed, norm_back = jax.vjp(normalize_round, wide_tokens)
    rolled = move_rows(normed, 3, 6, 1)
    labels_one = window_labels(
        region_labels(levels, lat_cells, lat_index * lat_cells, lat_cells * lat_devices),
        lon_cells,
        12,
    )

    def first_section(grid_field):
        return local_section(grid_field, first_inward, first_outward, labels_one, HEADS1)

    attended_rolled, first_back = jax.vjp(first_section, rolled)
    attended = move_rows(attended_rolled, 3, 6, -1)
    first_out = (wide_tokens + attended.astype(jnp.float32)).astype(jnp.bfloat16)
    merged_flat = merge_patches(first_out).reshape(-1, 4 * width_one)
    merged_norm, merge_back = jax.vjp(normalize_round, merged_flat.astype(jnp.float32))
    whole_merge = lax.all_gather(merge_weight, "lon", axis=0, tiled=True)
    reduced_sum = jnp.dot(merged_norm, whole_merge, preferred_element_type=jnp.float32)
    reduced = reduced_sum.astype(jnp.bfloat16).reshape(levels, half_rows, half_cols, width_two)
    reduced_wide = reduced.astype(jnp.float32)
    normed_two, norm_two_back = jax.vjp(normalize_round, reduced_wide)
    rolled_two = move_rows(normed_two, 3, 6, 1)
    triple = jnp.dot(
        rolled_two.reshape(-1, width_two), second_inward, preferred_element_type=jnp.float32
    ).astype(jnp.bfloat16)
    window_triple = to_windows(triple.reshape(levels, half_rows, half_cols, 3 * width_two), 6)
    queries = window_triple[..., :width_two]
    own_pair = window_triple[..., width_two:]
    far_pair = from_partner(own_pair, "lon", 0)
    labels_two = window_labels(
        region_labels(levels, half_rows, lat_index * half_rows, half_rows * lat_devices),
        half_cols,
        6,
    )
    key_labels = jnp.concatenate([labels_two, labels_two], axis=1)
    half_len = own_pair.shape[1]

    def second_core(query_part, pair_wide):
        blended = attend(
            query_part,
            pair_wide[..., :width_two],
            pair_wide[..., width_two:],
            labels_two,
            key_labels,
            HEADS2,
        )
        return jnp.dot(
            blended.reshape(-1, width_two), second_outward, preferred_element_type=jnp.float32
        ).astype(jnp.bfloat16)

    pair_all = jnp.concatenate([own_pair, far_pair], axis=1).astype(jnp.float32)
    projected, second_back = jax.vjp(second_core, queries, pair_all)
    number = queries.shape[0]
    attended_two_rolled = from_windows(
        projected.reshape(number, half_len, width_two), levels, half_rows, half_cols, 6
    )
    attended_two = move_rows(attended_two_rolled, 3, 6, -1)
    second_out = (reduced_wide + attended_two.astype(jnp.float32)).astype(jnp.bfloat16)
    grad_rolled_out = move_rows(cotangent, 3, 6, 1)
    grad_queries, grad_pair = second_back(to_windows(grad_rolled_out, 6).reshape(-1, width_two))
    grad_own_pair = grad_pair[:, :half_len]
    grad_far_pair = grad_pair[:, half_len:]
    returned = from_partner(grad_far_pair.astype(jnp.bfloat16), "lon", 0).astype(
        grad_far_pair.dtype
    )
    grad_triple = jnp.concatenate(
        [grad_queries, (grad_own_pair + returned).astype(jnp.bfloat16)], axis=-1
    )
    grad_flat = from_windows(grad_triple, levels, half_rows, half_cols, 6).reshape(
        -1, 3 * width_two
    )
    grad_rolled_two = jnp.einsum(
        "td,cd->tc", grad_flat, second_inward, preferred_element_type=jnp.float32
    ).astype(jnp.bfloat16)
    grad_normed_two = move_rows(
        grad_rolled_two.reshape(levels, half_rows, half_cols, width_two), 3, 6, -1
    )
    grad_reduced = (norm_two_back(grad_normed_two)[0] + cotangent.astype(jnp.float32)).astype(
        jnp.bfloat16
    )
    grad_reduced_flat = grad_reduced.reshape(-1, width_two)
    grad_merge_norm = jnp.einsum(
        "tc,rc->tr", grad_reduced_flat, whole_merge, preferred_element_type=jnp.float32
    ).astype(jnp.bfloat16)
    grad_merged = merge_back(grad_merge_norm)[0].astype(jnp.bfloat16)
    grad_first = grad_merged.reshape(levels, half_rows, half_cols, 2, 2, width_one).transpose(
        0, 1, 3, 2, 4, 5
    )
    grad_first = grad_first.reshape(levels, lat_cells, lon_cells, width_one)
    grad_rolled_one = move_rows(grad_first, 3, 6, 1)
    grad_rolled_in = first_back(grad_rolled_one)[0]
    grad_normed = move_rows(grad_rolled_in, 3, 6, -1)
    token_grad = (norm_back(grad_normed)[0] + grad_first.astype(jnp.float32)).astype(jnp.bfloat16)
    return (second_out, token_grad)


def solution(mesh):
    placed = (
        P(None, "lat", "lon", None),
        P(None, "lat", "lon", None),
        P(),
        P(),
        P("lon", None),
        P(),
        P(),
    )
    return jax.shard_map(
        local,
        mesh=mesh,
        in_specs=placed,
        out_specs=(P(None, "lat", "lon", None), P(None, "lat", "lon", None)),
        check_vma=False,
    )
```

profile of v0, /device:TPU:2, one launch (start us, length us, event | category | flops | bytes accessed | tf_op | source)
XLA Modules:
  0.0 296.3 jit_solution(6889374749580586641)
XLA Ops:
  9.4 1.7 fusion.24
  14.2 2.3 collective-permute-start
  18.0 2.9 collective-permute-done
  22.0 3.4 %collective-permute-start.1 = (bf16[4,12,6,512]{3,0,2,1:T(4,128)(2,1)S(1)}, bf16[4,12,6,512]{3,0,2,1:T(4,128)(2,1)S(1)}, u32[]{:S(2)}, u32[]{:S(2)}) collective-permute-start(bf16[4,12,6,512]{3,0,2,1:T(4,128)(2,1)S(1)} %get-tuple-element.30), channel_id=1, source_target_pairs={{0,15},{1,0},{2,1},{3,2},{4,3},{5,4},{6,5},{7,6},{8,7},{9,8},{10,9... | collective-permute-start | bytes 884744 | tf_op jit(solution)/shard_map/ppermute | solution.py:16
  26.4 6.1 %collective-permute-done.1 = bf16[4,12,6,512]{3,0,2,1:T(4,128)(2,1)S(1)} collective-permute-done((bf16[4,12,6,512]{3,0,2,1:T(4,128)(2,1)S(1)}, bf16[4,12,6,512]{3,0,2,1:T(4,128)(2,1)S(1)}, u32[]{:S(2)}, u32[]{:S(2)}) %collective-permute-start.1) | collective-permute-done | bytes 294944 | tf_op jit(solution)/shard_map/ppermute | solution.py:16
  37.9 2.7 convolution_convert_fusion.1
  41.7 2.2 copy.129
  43.9 2.2 copy.130
  47.4 2.9 fusion.7
  54.0 1.8 copy.132
  55.8 2.3 convert_element_type.227
  58.1 2.4 convolution_convert_fusion.11
  63.1 2.1 reshape.352
  65.7 1.9 collective-permute-start.2
  67.7 3.9 %collective-permute-done.2 = bf16[4,3,12,512]{3,0,2,1:T(4,128)(2,1)S(1)} collective-permute-done((bf16[4,3,12,512]{3,0,2,1:T(4,128)(2,1)S(1)}, bf16[4,3,12,512]{3,0,2,1:T(4,128)(2,1)S(1)}, u32[]{:S(2)}, u32[]{:S(2)}) %collective-permute-start.2) | collective-permute-done | bytes 147488 | tf_op jit(solution)/shard_map/ppermute | solution.py:16
  74.3 4.8 %collective-permute-start.9 = (bf16[4,3,6,1024]{3,0,2,1:T(4,128)(2,1)}, bf16[4,3,6,1024]{3,0,2,1:T(4,128)(2,1)}, u32[]{:S(2)}, u32[]{:S(2)}) collective-permute-start(bf16[4,3,6,1024]{3,0,2,1:T(4,128)(2,1)} %get-tuple-element.32), channel_id=1, source_target_pairs={{0,240},{16,0},{32,16},{48,32},{64,48},{80,64},{96,80},{112,96},{1... | collective-permute-start | bytes 442376 | tf_op jit(solution)/shard_map/ppermute | solution.py:16
  79.1 3.6 %collective-permute-done.3 = bf16[4,12,6,512]{3,0,2,1:T(4,128)(2,1)S(1)} collective-permute-done((bf16[4,12,6,512]{3,0,2,1:T(4,128)(2,1)S(1)}, bf16[4,12,6,512]{3,0,2,1:T(4,128)(2,1)S(1)}, u32[]{:S(2)}, u32[]{:S(2)}) %collective-permute-start.3) | collective-permute-done | bytes 294944 | tf_op jit(solution)/shard_map/ppermute | solution.py:16
  83.4 1.7 copy.183
  86.0 2.3 multiply_reduce_fusion.1
  88.3 3.2 %reshape.368 = f32[144,2048]{1,0:T(8,128)} reshape(f32[4,6,6,2,2,512]{5,4,3,2,1,0:T(2,128)} %bitcast.130) | data formatting | bytes 2359296 | tf_op jit(solution)/shard_map/convert_element_type | solution.py:154
  91.5 4.2 %fusion.61 = (f32[144]{0:T(256)S(1)}, f32[144,1024]{1,0:T(8,128)}) fusion(bf16[2048,1024]{1,0:T(8,128)(2,1)} %all-gather.2.cloned.1.call-done, f32[144,2048]{1,0:T(8,128)} %reshape.368, f32[144]{0:T(256)S(1)} %rsqrt.31, f32[144]{0:T(256)S(1)} %div.107), kind=kOutput, calls=%fused_computation.170 | convolution fusion | flops 605306752 | bytes 5965504 | tf_op jit(solution)/shard_map/dot_general | solution.py:156
  99.4 7.3 %collective-permute-start.4 = (bf16[4,3,6,1024]{3,2,1,0:T(8,128)(2,1)}, bf16[4,3,6,1024]{3,2,1,0:T(8,128)(2,1)}, u32[]{:S(2)}, u32[]{:S(2)}) collective-permute-start(bf16[4,3,6,1024]{3,2,1,0:T(8,128)(2,1)} %get-tuple-element.38), channel_id=1, source_target_pairs={{0,240},{16,0},{32,16},{48,32},{64,48},{80,64},{96,80},{112,96},{1... | collective-permute-start | bytes 442376 | tf_op jit(solution)/shard_map/ppermute | solution.py:16
  106.7 3.5 %collective-permute-done.4 = bf16[4,3,6,1024]{3,2,1,0:T(8,128)(2,1)} collective-permute-done((bf16[4,3,6,1024]{3,2,1,0:T(8,128)(2,1)}, bf16[4,3,6,1024]{3,2,1,0:T(8,128)(2,1)}, u32[]{:S(2)}, u32[]{:S(2)}) %collective-permute-start.4) | collective-permute-done | bytes 147488 | tf_op jit(solution)/shard_map/ppermute | solution.py:16
  110.2 1.8 pad_maximum_fusion.8
  112.3 1.9 pad_maximum_fusion.12
  114.2 3.5 %collective-permute-done.5 = bf16[4,6,6,1024]{3,2,1,0:T(8,128)(2,1)} collective-permute-done((bf16[4,6,6,1024]{3,2,1,0:T(8,128)(2,1)}, bf16[4,6,6,1024]{3,2,1,0:T(8,128)(2,1)}, u32[]{:S(2)}, u32[]{:S(2)}) %collective-permute-start.5) | collective-permute-done | bytes 294944 | tf_op jit(solution)/shard_map/ppermute | solution.py:16
  117.7 1.8 reshape.353
  119.5 4.0 %convolution_convert_fusion = bf16[144,3072]{1,0:T(8,128)(2,1)S(1)} fusion(bf16[144,1024]{1,0:T(8,128)(2,1)} %reshape.353, bf16[1024,3072]{1,0:T(8,128)(2,1)} %param.12), kind=kOutput, calls=%fused_computation.11 | convolution fusion | flops 906412032 | bytes 7471104 | tf_op jit(solution)/shard_map/dot_general | solution.py:161
  125.6 1.8 copy.139
  127.5 1.8 reshape_reshape_transpose_reshape.6
  129.3 2.5 convolution_convert_fusion.15
  131.8 2.2 reshape.357
  134.0 2.3 copy.140
  136.3 1.7 slice.249
  138.0 2.0 copy.136
  140.0 2.3 pad_maximum_fusion.3
  142.3 2.3 copy.137
  144.6 3.6 %fusion.20 = (f32[2,16,72]{2,1,0:T(8,128)S(1)}, f32[2,16,72,144]{3,2,1,0:T(8,128)}) fusion(pred[2,72,144]{2,1,0:T(8,128)(4,1)S(1)} %broadcast_compare_fusion.1, bf16[2,72,16,64]{1,3,2,0:T(8,128)(2,1)} %bitcast.150, bf16[2,144,16,64]{1,3,2,0:T(8,128)(2,1)} %bitcast.133), kind=kOutput, calls=%fused_computation.41 | convolution fusion | flops 43460352 | bytes 2241792 | tf_op jit(solution)/shard_map/jvp(nqhd,nkhd->nhqk)/dot_general | solution.py:65
  149.3 2.2 copy.135
  151.5 5.1 %fusion.14 = (f32[2,16,72]{2,1,0:T(8,128)}, bf16[2,16,72,144]{3,2,1,0:T(8,128)(2,1)S(1)}, bf16[2,16,72,144]{3,2,1,0:T(8,128)(2,1)}) fusion(f32[2,16,72,144]{3,2,1,0:T(8,128)} %get-tuple-element.44, f32[2,16,72]{2,1,0:T(8,128)} %multiply_divide_fusion.1, pred[2,72,144]{2,1,0:T(8,128)(4,1)S(1)} %broadcast_compare_fusion.1, f32[2,16,72]{2,1,0:T(8,128)} %copy-done.36, ...), kind=kOutput, calls=%fused_computation.23 | convolution fusion | flops 45451008 | bytes 3587328 | tf_op jit(solution)/shard_map/transpose(jvp(nhqk,nkhd->nqhd))/dot_general | solution.py:69
  157.8 1.8 fusion.62
  159.6 2.3 copy.138
  161.9 2.2 convert_element_type.247
  164.8 4.6 %fusion.49 = f32[2,16,144,64]{2,3,1,0:T(8,128)} fusion(bf16[2,72,16,64]{1,3,2,0:T(8,128)(2,1)} %bitcast.151, bf16[2,16,72,144]{3,2,1,0:T(8,128)(2,1)} %get-tuple-element.45, f32[2,16,72,144]{3,2,1,0:T(8,128)} %get-tuple-element.44, f32[2,16,72]{2,1,0:T(8,128)S(1)} %neg.21, f32[2,16,72]{2,1,0:T(8,128)} %copy-done.36, ...), kind=kOutput, calls=%fused_computation.162 | convolution fusion | flops 44789760 | bytes 3504384 | tf_op jit(solution)/shard_map/transpose(jvp(nqhd,nkhd->nhqk))/dot_general | solution.py:65
  169.4 2.7 copy.143
  172.1 2.7 copy.142
  174.7 2.2 fusion.31
  179.5 3.5 %convolution_convert_fusion.12 = bf16[2,16,72,64]{2,3,1,0:T(8,128)(2,1)S(1)} fusion(bf16[2,144,16,64]{1,3,2,0:T(8,128)(2,1)} %bitcast.134, bf16[2,16,72,144]{3,2,1,0:T(8,128)(2,1)} %get-tuple-element.45, f32[2,16,72,144]{3,2,1,0:T(8,128)} %get-tuple-element.44, f32[2,16,72]{2,1,0:T(8,128)} %copy-done.37, f32[2,16,72]{2,1,0:T(8,128)} %copy-done.36, ...), kind=kOutput, calls=%fused_computation.51 | convolution fusion | flops 44937216 | bytes 2914560 | tf_op jit(solution)/shard_map/transpose(jvp(nqhd,nkhd->nhqk))/dot_general | solution.py:65
  184.7 5.0 %convolution_convert_fusion.14 = bf16[144,1024]{1,0:T(8,128)(2,1)S(1)} fusion(bf16[144,3072]{1,0:T(8,128)(2,1)S(1)} %bitcast.140, bf16[1024,3072]{1,0:T(8,128)(2,1)} %param.12), kind=kOutput, calls=%fused_computation.54 | convolution fusion | flops 906117120 | bytes 7471104 | tf_op jit(solution)/shard_map/td,cd->tc/dot_general | solution.py:210
  190.8 6.8 %collective-permute-done.12 = bf16[4,3,6,1024]{3,2,1,0:T(8,128)(2,1)S(1)} collective-permute-done((bf16[4,3,6,1024]{3,2,1,0:T(8,128)(2,1)S(1)}, bf16[4,3,6,1024]{3,2,1,0:T(8,128)(2,1)S(1)}, u32[]{:S(2)}, u32[]{:S(2)}) %collective-permute-start.12) | collective-permute-done | bytes 147488 | tf_op jit(solution)/shard_map/ppermute | solution.py:16
  198.4 7.7 %collective-permute-done.7 = bf16[4,3,6,1024]{3,2,1,0:T(8,128)(2,1)S(1)} collective-permute-done((bf16[4,3,6,1024]{3,2,1,0:T(8,128)(2,1)S(1)}, bf16[4,3,6,1024]{3,2,1,0:T(8,128)(2,1)S(1)}, u32[]{:S(2)}, u32[]{:S(2)}) %collective-permute-start.7) | collective-permute-done | bytes 147488 | tf_op jit(solution)/shard_map/ppermute | solution.py:16
  206.5 2.5 collective-permute-done.13
  209.6 11.8 %collective-permute-done.8 = bf16[4,6,6,1024]{3,2,1,0:T(8,128)(2,1)S(1)} collective-permute-done((bf16[4,6,6,1024]{3,2,1,0:T(8,128)(2,1)S(1)}, bf16[4,6,6,1024]{3,2,1,0:T(8,128)(2,1)S(1)}, u32[]{:S(2)}, u32[]{:S(2)}) %collective-permute-start.8) | collective-permute-done | bytes 294944 | tf_op jit(solution)/shard_map/ppermute | solution.py:16
  223.6 3.8 %multiply_reduce_fusion = (f32[144]{0:T(256)S(1)}, f32[144,2048]{1,0:T(8,128)S(1)}) fusion(f32[144,2048]{1,0:T(8,128)S(1)} %copy-done.4, f32[144]{0:T(256)S(1)} %div.107, bf16[144,1024]{1,0:T(8,128)(2,1)S(1)} %reshape.360, bf16[2048,1024]{1,0:T(8,128)(2,1)} %all-gather.2.cloned.1.call-done), kind=kOutput, calls=%fused_computation.75 | convolution fusion | flops 605454208 | bytes 6849664 | tf_op jit(solution)/shard_map/tc,rc->tr/dot_general | solution.py:220
  231.4 6.1 %collective-permute-done.14 = bf16[4,3,12,512]{3,2,1,0:T(8,128)(2,1)S(1)} collective-permute-done((bf16[4,3,12,512]{3,2,1,0:T(8,128)(2,1)S(1)}, bf16[4,3,12,512]{3,2,1,0:T(8,128)(2,1)S(1)}, u32[]{:S(2)}, u32[]{:S(2)}) %collective-permute-start.14) | collective-permute-done | bytes 147488 | tf_op jit(solution)/shard_map/ppermute | solution.py:16
  238.4 5.3 %collective-permute-done.15 = bf16[4,12,6,512]{3,2,1,0:T(8,128)(2,1)S(1)} collective-permute-done((bf16[4,12,6,512]{3,2,1,0:T(8,128)(2,1)S(1)}, bf16[4,12,6,512]{3,2,1,0:T(8,128)(2,1)S(1)}, u32[]{:S(2)}, u32[]{:S(2)}) %collective-permute-start.15) | collective-permute-done | bytes 294944 | tf_op jit(solution)/shard_map/ppermute | solution.py:16
  246.9 1.7 reshape.364
  248.6 3.0 %convolution_convert_fusion.7 = bf16[4,8,64,144]{3,2,1,0:T(8,128)(2,1)S(1)} fusion(bf16[4,8,144,144]{2,3,1,0:T(8,128)(2,1)} %copy-done.3, bf16[4,8,64,144]{3,0,2,1:T(4,128)(2,1)} %bitcast.136), kind=kOutput, calls=%fused_computation.44 | convolution fusion | flops 85229568 | bytes 2506752 | tf_op jit(solution)/shard_map/transpose(jvp(nhqk,nkhd->nqhd))/dot_general | solution.py:69
  251.6 4.5 %fusion.5 = (f32[4,8,144]{2,1,0:T(8,128)S(1)}, bf16[4,8,144,144]{2,3,1,0:T(8,128)(2,1)S(1)}) fusion(f32[4,8,144,144]{2,3,1,0:T(8,128)} %copy-done.7, f32[4,8,144]{2,1,0:T(8,128)S(1)} %multiply_divide_fusion, pred[4,144,144]{1,2,0:T(8,128)(4,1)S(1)} %copy-done.28, bf16[4,144,8,64]{1,3,2,0:T(8,128)(2,1)S(1)} %bitcast.132, bf16[4,8,64,144]{3,0,2,1:T(4,128)(2,1)} %bitcast.137), kind=kOutput, calls=%fused_computation.7 | convolution fusion | flops 89574912 | bytes 5280768 | tf_op jit(solution)/shard_map/transpose(jvp(nhqk,nkhd->nqhd))/dot_general | solution.py:69
  256.2 3.0 convolution_convert_fusion.6
  259.2 2.8 convolution_convert_fusion.5
  269.8 5.0 %collective-permute-done.16 = bf16[4,3,12,512]{3,0,2,1:T(4,128)(2,1)S(1)} collective-permute-done((bf16[4,3,12,512]{3,0,2,1:T(4,128)(2,1)S(1)}, bf16[4,3,12,512]{3,0,2,1:T(4,128)(2,1)S(1)}, u32[]{:S(2)}, u32[]{:S(2)}) %collective-permute-start.16) | collective-permute-done | bytes 147488 | tf_op jit(solution)/shard_map/ppermute | solution.py:16
  276.6 8.8 %collective-permute-done.17 = bf16[4,12,6,512]{3,0,2,1:T(4,128)(2,1)S(1)} collective-permute-done((bf16[4,12,6,512]{3,0,2,1:T(4,128)(2,1)S(1)}, bf16[4,12,6,512]{3,0,2,1:T(4,128)(2,1)S(1)}, u32[]{:S(2)}, u32[]{:S(2)}) %collective-permute-start.17) | collective-permute-done | bytes 294944 | tf_op jit(solution)/shard_map/ppermute | solution.py:16
  287.4 1.9 fusion.32
  (234 shorter events, 65.4 us)
Async XLA Ops:
  7.2 122.1 %copy-start = (bf16[1024,1024]{1,0:T(8,128)(2,1)S(1)}, bf16[1024,1024]{1,0:T(8,128)(2,1)}, u32[]{:S(2)}) copy-start(bf16[1024,1024]{1,0:T(8,128)(2,1)} %param.13) | copy-start | bytes 6291460
  7.2 4.5 %copy-start.2 = (bf16[4,12,12,512]{3,0,2,1:T(4,128)(2,1)S(1)}, bf16[4,12,12,512]{3,0,2,1:T(4,128)(2,1)}, u32[]{:S(2)}) copy-start(bf16[4,12,12,512]{3,0,2,1:T(4,128)(2,1)} %param.7) | copy-start | bytes 1769476
  7.2 84.3 %all-gather.2.cloned.1.call-start = ((), (), s32[]{:S(2)}) async-start(), calls=%async_computation | async-start | bytes 4456448 | tf_op jit(solution)/shard_map/all_gather | solution.py:155
  9.4 3.1 %copy-start.11 = (f32[4,12,12]{0,2,1:T(8,128)}, f32[4,12,12]{0,2,1:T(8,128)S(1)}, u32[]{:S(2)}) copy-start(f32[4,12,12]{0,2,1:T(8,128)S(1)} %broadcast_multiply_fusion) | copy-start | bytes 6916
  11.1 0.6 copy-start.25
  11.7 2.5 copy-start.18
  12.7 0.7 copy-start.14
  14.2 6.7 %collective-permute-start = (bf16[4,3,12,512]{3,0,2,1:T(4,128)(2,1)}, bf16[4,3,12,512]{3,0,2,1:T(4,128)(2,1)S(1)}, u32[]{:S(2)}, u32[]{:S(2)}) collective-permute-start(bf16[4,3,12,512]{3,0,2,1:T(4,128)(2,1)} %pad_maximum_fusion.17), channel_id=1, source_target_pairs={{0,240},{16,0},{32,16},{48,32},{64,48},{80,64},{96,80},{112,96},{1... | collective-permute-start | bytes 442376 | tf_op jit(solution)/shard_map/ppermute | solution.py:16
  22.0 10.5 %collective-permute-start.1 = (bf16[4,12,6,512]{3,0,2,1:T(4,128)(2,1)S(1)}, bf16[4,12,6,512]{3,0,2,1:T(4,128)(2,1)S(1)}, u32[]{:S(2)}, u32[]{:S(2)}) collective-permute-start(bf16[4,12,6,512]{3,0,2,1:T(4,128)(2,1)S(1)} %get-tuple-element.30), channel_id=1, source_target_pairs={{0,15},{1,0},{2,1},{3,2},{4,3},{5,4},{6,5},{7,6},{8,7},{9,8},{10,9... | collective-permute-start | bytes 884744 | tf_op jit(solution)/shard_map/ppermute | solution.py:16
  32.5 0.7 copy-start.31
  43.9 3.5 %copy-start.27 = (pred[4,144,144]{1,2,0:T(8,128)(4,1)S(1)}, pred[4,144,144]{1,2,0:T(8,128)(4,1)}, u32[]{:S(2)}) copy-start(pred[4,144,144]{1,2,0:T(8,128)(4,1)} %broadcast_compare_fusion) | copy-start | bytes 248836
  50.4 2.2 copy-start.7
  50.4 2.2 copy-start.34
  50.4 2.2 copy-start.8
  52.6 1.4 copy-start.3
  65.6 7.4 %copy-start.16 = (bf16[4,6,6,1024]{3,0,2,1:T(4,128)(2,1)S(1)}, bf16[4,6,6,1024]{3,0,2,1:T(4,128)(2,1)}, u32[]{:S(2)}) copy-start(bf16[4,6,6,1024]{3,0,2,1:T(4,128)(2,1)} %param.8) | copy-start | bytes 884740
  65.7 5.9 %collective-permute-start.2 = (bf16[4,3,12,512]{3,0,2,1:T(4,128)(2,1)S(1)}, bf16[4,3,12,512]{3,0,2,1:T(4,128)(2,1)S(1)}, u32[]{:S(2)}, u32[]{:S(2)}) collective-permute-start(bf16[4,3,12,512]{3,0,2,1:T(4,128)(2,1)S(1)} %pad_maximum_fusion.16), channel_id=1, source_target_pairs={{0,16},{16,32},{32,48},{48,64},{64,80},{80,96},{96,112},{112,128},... | collective-permute-start | bytes 442376 | tf_op jit(solution)/shard_map/ppermute | solution.py:16
  72.3 10.4 %collective-permute-start.3 = (bf16[4,12,6,512]{3,0,2,1:T(4,128)(2,1)S(1)}, bf16[4,12,6,512]{3,0,2,1:T(4,128)(2,1)S(1)}, u32[]{:S(2)}, u32[]{:S(2)}) collective-permute-start(bf16[4,12,6,512]{3,0,2,1:T(4,128)(2,1)S(1)} %get-tuple-element.27), channel_id=1, source_target_pairs={{0,1},{1,2},{2,3},{3,4},{4,5},{5,6},{6,7},{7,8},{8,9},{9,10},{10,1... | collective-permute-start | bytes 884744 | tf_op jit(solution)/shard_map/ppermute | solution.py:16
  74.3 38.0 %collective-permute-start.9 = (bf16[4,3,6,1024]{3,0,2,1:T(4,128)(2,1)}, bf16[4,3,6,1024]{3,0,2,1:T(4,128)(2,1)}, u32[]{:S(2)}, u32[]{:S(2)}) collective-permute-start(bf16[4,3,6,1024]{3,0,2,1:T(4,128)(2,1)} %get-tuple-element.32), channel_id=1, source_target_pairs={{0,240},{16,0},{32,16},{48,32},{64,48},{80,64},{96,80},{112,96},{1... | collective-permute-start | bytes 442376 | tf_op jit(solution)/shard_map/ppermute | solution.py:16
  83.4 1.7 copy-start.6
  88.3 7.4 %copy-start.38 = (f32[144]{0:T(256)}, f32[144]{0:T(256)S(1)}, u32[]{:S(2)}) copy-start(f32[144]{0:T(256)S(1)} %rsqrt.31) | copy-start | bytes 1732
  98.3 13.8 %copy-start.32 = (f32[4,6,6]{2,1,0:T(8,128)}, f32[4,6,6]{2,1,0:T(8,128)S(1)}, u32[]{:S(2)}) copy-start(f32[4,6,6]{2,1,0:T(8,128)S(1)} %add.140) | copy-start | bytes 1732
  99.4 10.8 %collective-permute-start.4 = (bf16[4,3,6,1024]{3,2,1,0:T(8,128)(2,1)}, bf16[4,3,6,1024]{3,2,1,0:T(8,128)(2,1)}, u32[]{:S(2)}, u32[]{:S(2)}) collective-permute-start(bf16[4,3,6,1024]{3,2,1,0:T(8,128)(2,1)} %get-tuple-element.38), channel_id=1, source_target_pairs={{0,240},{16,0},{32,16},{48,32},{64,48},{80,64},{96,80},{112,96},{1... | collective-permute-start | bytes 442376 | tf_op jit(solution)/shard_map/ppermute | solution.py:16
  112.1 5.6 %collective-permute-start.5 = (bf16[4,6,6,1024]{3,2,1,0:T(8,128)(2,1)}, bf16[4,6,6,1024]{3,2,1,0:T(8,128)(2,1)}, u32[]{:S(2)}, u32[]{:S(2)}) collective-permute-start(bf16[4,6,6,1024]{3,2,1,0:T(8,128)(2,1)} %pad_maximum_fusion.8), channel_id=1, source_target_pairs={{0,15},{1,0},{2,1},{3,2},{4,3},{5,4},{6,5},{7,6},{8,7},{9,8},{10,9... | collective-permute-start | bytes 884744 | tf_op jit(solution)/shard_map/ppermute | solution.py:16
  114.2 11.4 %collective-permute-start.10 = (bf16[4,6,6,1024]{3,0,2,1:T(4,128)(2,1)}, bf16[4,6,6,1024]{3,0,2,1:T(4,128)(2,1)}, u32[]{:S(2)}, u32[]{:S(2)}) collective-permute-start(bf16[4,6,6,1024]{3,0,2,1:T(4,128)(2,1)} %pad_maximum_fusion.12), channel_id=1, source_target_pairs={{0,15},{1,0},{2,1},{3,2},{4,3},{5,4},{6,5},{7,6},{8,7},{9,8},{10,9... | collective-permute-start | bytes 884744 | tf_op jit(solution)/shard_map/ppermute | solution.py:16
  123.5 0.9 copy-start.13
  125.3 14.7 %collective-permute-start.6 = (bf16[2,72,2048]{2,1,0:T(8,128)(2,1)}, bf16[2,72,2048]{2,1,0:T(8,128)(2,1)}, u32[]{:S(2)}, u32[]{:S(2)}) collective-permute-start(bf16[2,72,2048]{2,1,0:T(8,128)(2,1)} %slice.246), channel_id=1, source_target_pairs={{0,1},{1,0},{2,3},{3,2},{4,5},{5,4},{6,7},{7,6},{8,9},{9,8},{10,11... | collective-permute-start | bytes 1769480 | tf_op jit(solution)/shard_map/ppermute | solution.py:20
  148.1 0.6 copy-start.36
  151.5 5.1 %copy-start.10 = (bf16[2,144,1024]{1,2,0:T(8,128)(2,1)S(1)}, bf16[2,144,1024]{1,2,0:T(8,128)(2,1)}, u32[]{:S(2)}) copy-start(bf16[2,144,1024]{1,2,0:T(8,128)(2,1)} %copy.135) | copy-start | bytes 1769476
  156.6 1.3 copy-start.15
  164.8 4.6 %copy-start.37 = (f32[2,16,72]{2,1,0:T(8,128)}, f32[2,16,72]{2,1,0:T(8,128)S(1)}, u32[]{:S(2)}) copy-start(f32[2,16,72]{2,1,0:T(8,128)S(1)} %neg.21) | copy-start | bytes 27652
  174.7 2.9 copy-start.22
  176.9 6.3 %collective-permute-start.11 = (bf16[2,72,2048]{2,1,0:T(8,128)(2,1)}, bf16[2,72,2048]{2,1,0:T(8,128)(2,1)}, u32[]{:S(2)}, u32[]{:S(2)}) collective-permute-start(bf16[2,72,2048]{2,1,0:T(8,128)(2,1)} %fusion.31), channel_id=1, source_target_pairs={{0,1},{1,0},{2,3},{3,2},{4,5},{5,4},{6,7},{7,6},{8,9},{9,8},{10,11... | collective-permute-start | bytes 1769480 | tf_op jit(solution)/shard_map/ppermute | solution.py:20
  178.1 0.7 copy-start.21
  179.5 3.8 %copy-start.5 = (f32[2,144,1024]{2,1,0:T(8,128)S(1)}, f32[2,144,1024]{2,1,0:T(8,128)}, u32[]{:S(2)}) copy-start(f32[2,144,1024]{2,1,0:T(8,128)} %copy.143) | copy-start | bytes 3538948
  189.7 0.9 copy-start.30
  189.7 1.0 slice-start.2
  190.0 7.7 %collective-permute-start.12 = (bf16[4,3,6,1024]{3,2,1,0:T(8,128)(2,1)S(1)}, bf16[4,3,6,1024]{3,2,1,0:T(8,128)(2,1)S(1)}, u32[]{:S(2)}, u32[]{:S(2)}) collective-permute-start(bf16[4,3,6,1024]{3,2,1,0:T(8,128)(2,1)S(1)} %get-tuple-element.33), channel_id=1, source_target_pairs={{0,16},{16,32},{32,48},{48,64},{64,80},{80,96},{96,112},{112,128},... | collective-permute-start | bytes 442376 | tf_op jit(solution)/shard_map/ppermute | solution.py:16
  197.6 11.6 %copy-start.33 = (f32[4,6,6]{2,1,0:T(8,128)S(1)}, f32[4,6,6]{2,1,0:T(8,128)}, u32[]{:S(2)}) copy-start(f32[4,6,6]{2,1,0:T(8,128)} %copy-done.32) | copy-start | bytes 1732
  197.7 11.2 %collective-permute-start.13 = (bf16[4,6,6,1024]{3,2,1,0:T(8,128)(2,1)S(1)}, bf16[4,6,6,1024]{3,2,1,0:T(8,128)(2,1)S(1)}, u32[]{:S(2)}, u32[]{:S(2)}) collective-permute-start(bf16[4,6,6,1024]{3,2,1,0:T(8,128)(2,1)S(1)} %pad_maximum_fusion.10), channel_id=1, source_target_pairs={{0,1},{1,2},{2,3},{3,4},{4,5},{5,6},{6,7},{7,8},{8,9},{9,10},{10,1... | collective-permute-start | bytes 884744 | tf_op jit(solution)/shard_map/ppermute | solution.py:16
  197.8 23.5 %copy-start.17 = (bf16[4,6,6,1024]{3,0,2,1:T(4,128)(2,1)S(1)}, bf16[4,6,6,1024]{3,0,2,1:T(4,128)(2,1)}, u32[]{:S(2)}) copy-start(bf16[4,6,6,1024]{3,0,2,1:T(4,128)(2,1)} %param.8) | copy-start | bytes 884740
  197.9 8.2 %collective-permute-start.7 = (bf16[4,3,6,1024]{3,2,1,0:T(8,128)(2,1)S(1)}, bf16[4,3,6,1024]{3,2,1,0:T(8,128)(2,1)S(1)}, u32[]{:S(2)}, u32[]{:S(2)}) collective-permute-start(bf16[4,3,6,1024]{3,2,1,0:T(8,128)(2,1)S(1)} %get-tuple-element.35), channel_id=1, source_target_pairs={{0,16},{16,32},{32,48},{48,64},{64,80},{80,96},{96,112},{112,128},... | collective-permute-start | bytes 442376 | tf_op jit(solution)/shard_map/ppermute | solution.py:16
  206.1 15.3 %collective-permute-start.8 = (bf16[4,6,6,1024]{3,2,1,0:T(8,128)(2,1)S(1)}, bf16[4,6,6,1024]{3,2,1,0:T(8,128)(2,1)S(1)}, u32[]{:S(2)}, u32[]{:S(2)}) collective-permute-start(bf16[4,6,6,1024]{3,2,1,0:T(8,128)(2,1)S(1)} %pad_maximum_fusion.9), channel_id=1, source_target_pairs={{0,1},{1,2},{2,3},{3,4},{4,5},{5,6},{6,7},{7,8},{8,9},{9,10},{10,1... | collective-permute-start | bytes 884744 | tf_op jit(solution)/shard_map/ppermute | solution.py:16
  209.6 14.0 %copy-start.4 = (f32[144,2048]{1,0:T(8,128)S(1)}, f32[144,2048]{1,0:T(8,128)}, u32[]{:S(2)}) copy-start(f32[144,2048]{1,0:T(8,128)} %reshape.368) | copy-start | bytes 3538948
  223.6 3.9 %copy-start.39 = (f32[144]{0:T(256)S(1)}, f32[144]{0:T(256)}, u32[]{:S(2)}) copy-start(f32[144]{0:T(256)} %copy-done.38) | copy-start | bytes 1732
  230.7 7.6 %copy-start.35 = (f32[4,8,144]{2,1,0:T(8,128)S(1)}, f32[4,8,144]{2,1,0:T(8,128)}, u32[]{:S(2)}) copy-start(f32[4,8,144]{2,1,0:T(8,128)} %copy-done.34) | copy-start | bytes 55300
  230.8 6.6 %collective-permute-start.14 = (bf16[4,3,12,512]{3,2,1,0:T(8,128)(2,1)S(1)}, bf16[4,3,12,512]{3,2,1,0:T(8,128)(2,1)S(1)}, u32[]{:S(2)}, u32[]{:S(2)}) collective-permute-start(bf16[4,3,12,512]{3,2,1,0:T(8,128)(2,1)S(1)} %slice.265), channel_id=1, source_target_pairs={{0,240},{16,0},{32,16},{48,32},{64,48},{80,64},{96,80},{112,96},{1... | collective-permute-start | bytes 442376 | tf_op jit(solution)/shard_map/ppermute | solution.py:16
  237.6 6.0 %collective-permute-start.15 = (bf16[4,12,6,512]{3,2,1,0:T(8,128)(2,1)S(1)}, bf16[4,12,6,512]{3,2,1,0:T(8,128)(2,1)S(1)}, u32[]{:S(2)}, u32[]{:S(2)}) collective-permute-start(bf16[4,12,6,512]{3,2,1,0:T(8,128)(2,1)S(1)} %get-tuple-element.20), channel_id=1, source_target_pairs={{0,15},{1,0},{2,1},{3,2},{4,3},{5,4},{6,5},{7,6},{8,7},{9,8},{10,9... | collective-permute-start | bytes 884744 | tf_op jit(solution)/shard_map/ppermute | solution.py:16
  243.9 1.0 copy-start.29
  246.8 4.8 %copy-start.9 = (bf16[4,144,512]{1,2,0:T(8,128)(2,1)S(1)}, bf16[4,144,512]{1,2,0:T(8,128)(2,1)}, u32[]{:S(2)}) copy-start(bf16[4,144,512]{1,2,0:T(8,128)(2,1)} %copy.128) | copy-start | bytes 1769476
  248.5 3.1 %copy-start.28 = (pred[4,144,144]{1,2,0:T(8,128)(4,1)S(1)}, pred[4,144,144]{1,2,0:T(8,128)(4,1)}, u32[]{:S(2)}) copy-start(pred[4,144,144]{1,2,0:T(8,128)(4,1)} %broadcast_compare_fusion) | copy-start | bytes 248836
  248.5 7.6 %slice-start = ((s8[4718592]{0:T(1024)(128)(4,1)}), s8[4194304]{0:T(1024)(128)(4,1)S(1)}, s32[]{:S(2)}) async-start(s8[4718592]{0:T(1024)(128)(4,1)} %bitcast.128), calls=%async_computation.1 | async-start | bytes 8388608
  251.6 4.6 %slice-start.1 = ((s8[4718592]{0:T(1024)(128)(4,1)}), s8[524288]{0:T(1024)(128)(4,1)S(1)}, s32[]{:S(2)}) async-start(s8[4718592]{0:T(1024)(128)(4,1)} %bitcast.128), calls=%async_computation.2 | async-start | bytes 1048576
  251.6 4.6 %copy-start.24 = (bf16[4,144,512]{1,2,0:T(8,128)(2,1)S(1)}, bf16[4,144,512]{1,2,0:T(8,128)(2,1)}, u32[]{:S(2)}) copy-start(bf16[4,144,512]{1,2,0:T(8,128)(2,1)} %copy.129) | copy-start | bytes 1769476
  256.2 3.0 %copy-start.23 = (bf16[4,144,512]{1,2,0:T(8,128)(2,1)S(1)}, bf16[4,144,512]{1,2,0:T(8,128)(2,1)}, u32[]{:S(2)}) copy-start(bf16[4,144,512]{1,2,0:T(8,128)(2,1)} %copy.130) | copy-start | bytes 1769476
  265.4 1.4 copy-start.40
  269.2 6.4 %copy-start.20 = (bf16[4,6,6,1024]{3,2,1,0:T(8,128)(2,1)S(1)}, bf16[4,6,6,1024]{3,2,1,0:T(8,128)(2,1)}, u32[]{:S(2)}) copy-start(bf16[4,6,6,1024]{3,2,1,0:T(8,128)(2,1)} %get-tuple-element.22) | copy-start | bytes 884740
  269.4 16.0 %copy-start.12 = (f32[4,12,12]{0,2,1:T(8,128)S(1)}, f32[4,12,12]{0,2,1:T(8,128)}, u32[]{:S(2)}) copy-start(f32[4,12,12]{0,2,1:T(8,128)} %copy-done.11) | copy-start | bytes 6916
  269.4 5.4 %collective-permute-start.16 = (bf16[4,3,12,512]{3,0,2,1:T(4,128)(2,1)S(1)}, bf16[4,3,12,512]{3,0,2,1:T(4,128)(2,1)S(1)}, u32[]{:S(2)}, u32[]{:S(2)}) collective-permute-start(bf16[4,3,12,512]{3,0,2,1:T(4,128)(2,1)S(1)} %pad_maximum_fusion.14), channel_id=1, source_target_pairs={{0,16},{16,32},{32,48},{48,64},{64,80},{80,96},{96,112},{112,128},... | collective-permute-start | bytes 442376 | tf_op jit(solution)/shard_map/ppermute | solution.py:16
  275.3 10.8 %copy-start.26 = (f32[4,12,12]{0,2,1:T(8,128)S(1)}, f32[4,12,12]{0,2,1:T(8,128)}, u32[]{:S(2)}) copy-start(f32[4,12,12]{0,2,1:T(8,128)} %copy-done.25) | copy-start | bytes 6916
  275.3 10.9 %copy-start.19 = (f32[4,12,12]{0,2,1:T(8,128)S(1)}, f32[4,12,12]{0,2,1:T(8,128)}, u32[]{:S(2)}) copy-start(f32[4,12,12]{0,2,1:T(8,128)} %copy-done.18) | copy-start | bytes 6916
  275.6 9.8 %collective-permute-start.17 = (bf16[4,12,6,512]{3,0,2,1:T(4,128)(2,1)S(1)}, bf16[4,12,6,512]{3,0,2,1:T(4,128)(2,1)S(1)}, u32[]{:S(2)}, u32[]{:S(2)}) collective-permute-start(bf16[4,12,6,512]{3,0,2,1:T(4,128)(2,1)S(1)} %get-tuple-element.23), channel_id=1, source_target_pairs={{0,1},{1,2},{2,3},{3,4},{4,5},{5,6},{6,7},{7,8},{8,9},{9,10},{10,1... | collective-permute-start | bytes 884744 | tf_op jit(solution)/shard_map/ppermute | solution.py:16
  286.2 3.1 %copy-start.1 = (bf16[1024,1024]{1,0:T(8,128)(2,1)S(1)}, bf16[1024,1024]{1,0:T(8,128)(2,1)}, u32[]{:S(2)}) copy-start(bf16[1024,1024]{1,0:T(8,128)(2,1)} %param.13) | copy-start | bytes 6291460
Sparse Core Ops, SparseCore 0:
  10.8 62.9 all-gather.1
where the time goes:
time: 302 us; the launch traced here: 296 us
  waiting for transfers between devices  78 us (26%)
  local copies, waits for them, and re-layouts  77.8 us (26%)
  matrix products  64.2 us (21%)
  other arithmetic  36.9 us (12%)
  starting transfers between devices  24 us (8%)
  between operations  15.4 us (5%)
    ppermute x16, waiting for transfers between devices, from_behind(): return lax.ppermute(value, axis, pairs)  77.4 us
    ppermute x16, starting transfers between devices, from_behind(): return lax.ppermute(value, axis, pairs)  23.2 us
    dot_general x6, matrix products, attend(): jnp.einsum('nqhd,nkhd->nhqk', query_heads, key_heads) * head_size ** (-0.5)  20.4 us
    dot_general x6, matrix products, attend(): jnp.einsum('nhqk,nkhd->nqhd', shares.astype(jnp.float32), value_heads)  16.1 us
    unnamed x90, local copies, waits for them, and re-layouts  9.28 us
    convert_element_type x4, local copies, waits for them, and re-layouts, attend(): return blended.reshape(number, query_len, channels).astype(jnp.bfloat16)  8.61 us
    concatenate x10, other arithmetic, move_rows(): jnp.concatenate([remain, arrived] if direction == 1 else [arrived, remain...  7.91 us
  transfers between devices with their start and end apart: 19, of which 14 were waited for; matrix products, arithmetic and copies ran while one was open for 30% of the time, Pallas kernels for 0%

commit v1 on v0

v1 whole, which is shorter than its diff:
```python
import functools

import jax
import jax.numpy as jnp
import numpy as np
from jax import lax
from jax.experimental import pallas as pl
from jax.experimental.pallas import tpu as pltpu
from jax.sharding import PartitionSpec as P

F32 = jnp.float32
BF = jnp.bfloat16
NT = ((1,), (1,))
TN = ((0,), (0,))
EPS = 1e-05
MESH = pl.DeviceIdType.MESH


def dot(a, b, dims=((1,), (0,))):
    return lax.dot_general(a, b, (dims, ((), ())), preferred_element_type=F32)


def window_place(level, row_half, counters):
    key = ("a", row_half) if level in (1, 2) else (level, row_half)
    start = {("a", 0): 0, ("a", 1): 72, (3, 0): 144, (3, 1): 180, (0, 0): 216, (0, 1): 252}[key]
    taken = counters.get(key, 0)
    counters[key] = taken + 1
    return start + taken


@functools.lru_cache(None)
def orders():
    raw = np.zeros((144, 192), np.float32)
    for h in range(2):
        for slab in range(12):
            for k in range(6):
                raw[h * 72 + slab * 6 + k, slab * 16 + 6 * h + k] = 1
    one = np.zeros((288, 288), np.float32)
    counters = {}
    for h in range(2):
        for g in range(2):
            for lev in range(4):
                for k in range(18):
                    one[window_place(lev, g, counters), (h * 2 + g) * 72 + lev * 18 + k] = 1
    two = np.zeros((288, 288), np.float32)
    counters = {}
    for m in range(2):
        for h in range(2):
            for lev in range(4):
                for i in range(6):
                    for j in range(3):
                        two[window_place(lev, i // 3, counters), m * 144 + h * 72 + lev * 18 + i * 3 + j] = 1
    merge = np.zeros((288, 288), np.float32)
    for p in range(2):
        for q in range(2):
            for lev in range(4):
                for i in range(6):
                    for j in range(3):
                        row, col = 2 * i + p, 2 * j + q
                        source = (row // 3) * 72 + lev * 18 + (row % 3) * 6 + col
                        merge[(p * 2 + q) * 72 + lev * 18 + i * 3 + j, source] = 1
    coarse = np.zeros((144, 192), np.float32)
    for h in range(2):
        for lev in range(4):
            for i in range(6):
                for j in range(3):
                    slab = ((i // 3) * 4 + lev) * 3 + i % 3
                    coarse[h * 72 + lev * 18 + i * 3 + j, slab * 8 + h * 3 + j] = 1
    mats = (raw, one, one.T, two, two.T, merge, merge.T, coarse, coarse.T)
    return tuple(np.asarray(m, dtype=BF) for m in mats)


def head_rows():
    lane = lax.broadcasted_iota(jnp.int32, (1, 256), 1)
    return [jnp.where((lane >= 64 * h) & (lane < 64 * h + 64), 1.0, 0.0).astype(BF) for h in range(4)]


def stack(x, rows):
    pad = jnp.zeros((16, 256), BF)
    parts = []
    for r in rows:
        parts += [x * r, pad]
    return jnp.concatenate(parts, axis=0)


def unstack(y):
    lane = lax.broadcasted_iota(jnp.int32, (144, 256), 1)
    out = y[480:624]
    for h in (2, 1, 0):
        out = jnp.where(lane < 64 * h + 64, y[160 * h : 160 * h + 144], out)
    return out


def attend(trip, mask, mixed, shares):
    rows = head_rows()
    for s in range(2):
        for g in range(2):
            r = pl.ds(144 * s, 144)
            q = trip[r, pl.ds(256 * g, 256)] * jnp.asarray(0.125, BF)
            k = trip[r, pl.ds(512 + 256 * g, 256)]
            v = trip[r, pl.ds(1024 + 256 * g, 256)]
            raised = jnp.exp(dot(k, stack(q, rows), NT) + mask[s])
            p = (raised * (1.0 / jnp.sum(raised, axis=0, keepdims=True))).astype(BF)
            shares[2 * s + g] = p
            mixed[r, pl.ds(256 * g, 256)] = unstack(dot(p, v, TN)).astype(BF)


def attend_back(trip, grad_mixed, shares, grad_trip):
    rows = head_rows()
    for s in range(2):
        for g in range(2):
            r = pl.ds(144 * s, 144)
            q = trip[r, pl.ds(256 * g, 256)] * jnp.asarray(0.125, BF)
            k = trip[r, pl.ds(512 + 256 * g, 256)]
            v = trip[r, pl.ds(1024 + 256 * g, 256)]
            do = stack(grad_mixed[r, pl.ds(256 * g, 256)], rows)
            p = shares[2 * s + g]
            wide = p.astype(F32)
            t = wide * dot(v, do, NT)
            ds = (t - wide * jnp.sum(t, axis=0, keepdims=True)).astype(BF)
            grad_trip[r, pl.ds(1024 + 256 * g, 256)] = dot(p, do).astype(BF)
            grad_trip[r, pl.ds(512 + 256 * g, 256)] = dot(ds, stack(q, rows)).astype(BF)
            grad_trip[r, pl.ds(256 * g, 256)] = (unstack(dot(ds, k, TN)) * 0.125).astype(BF)


def norm(x):
    center = x - jnp.mean(x, axis=-1, keepdims=True)
    scale = lax.rsqrt(jnp.mean(center * center, axis=-1, keepdims=True) + EPS)
    return center * scale, scale


def norm_back(grad, hat, scale):
    first = jnp.mean(grad, axis=-1, keepdims=True)
    second = jnp.mean(grad * hat, axis=-1, keepdims=True)
    return scale * (grad - first - hat * second)


SCRATCH = dict(
    raw=((4, 12, 12, 512), BF),
    own=((2, 4, 72, 512), BF),
    tok=((2, 4, 72, 512), BF),
    nrm=((2, 288, 512), BF),
    rs1=((2, 288, 128), F32),
    trip1=((2, 288, 1536), BF),
    ps1=((2, 4, 144, 640), BF),
    mix=((288, 512), BF),
    mk=((2, 2, 144, 640), F32),
    fo=((2, 4, 72, 512), BF),
    lay=((2, 4, 72, 512), BF),
    mf=((144, 2048), F32),
    mn=((144, 2048), BF),
    rsm=((144, 128), F32),
    red=((144, 1024), BF),
    nt=((2, 144, 1024), BF),
    rs2=((144, 128), F32),
    w1i_v=((512, 1536), BF),
    w1o_v=((512, 512), BF),
    wmv=((16, 128, 1024), BF),
    w2i_v=((1024, 1536), BF),
    w2o_v=((1024, 1024), BF),
    c_raw=((144, 192), BF),
    one=((288, 288), BF),
    one_t=((288, 288), BF),
    two=((288, 288), BF),
    two_t=((288, 288), BF),
    mer=((288, 288), BF),
    mer_t=((288, 288), BF),
    coa=((144, 192), BF),
    coa_t=((192, 144), BF),
    cot_r=((2, 4, 3, 6, 1024), BF),
    cot2=((2, 144, 1024), BF),
    trip2=((288, 1536), BF),
    ps2=((4, 144, 640), BF),
    mix2=((288, 512), BF),
    mxo=((144, 512), BF),
    mxs=((144, 512), BF),
    mxr=((144, 512), BF),
    dmix=((288, 512), BF),
    dmix2=((288, 512), BF),
    dtrip=((288, 1536), BF),
    pgs=((144, 1024), BF),
    pgr=((144, 1024), BF),
    pgo=((144, 1024), F32),
    gr=((144, 1024), BF),
    gmn=((144, 2048), BF),
    gf=((2, 4, 72, 512), BF),
    g1=((2, 4, 72, 512), BF),
    tg=((2, 4, 72, 512), BF),
    s2o=((2, 4, 3, 6, 1024), BF),
)
N_IN = 16
N_SEM = 80


class Remote:
    def __init__(self, copy, when):
        self.copy, self.when = copy, when

    def run(self, act, when):
        if when is None:
            act()
        else:
            pl.when(when)(act)

    def start(self):
        self.run(self.copy.start, self.when)

    def wait_send(self):
        self.run(self.copy.wait_send, self.when)

    def wait_recv(self, when=None):
        self.run(self.copy.wait_recv, self.when if when is None else when)


class Copies:
    def __init__(self, local, send, recv):
        self.local_sems, self.send_sems, self.recv_sems = local, send, recv
        self.locals, self.remotes = 0, []

    def local(self, source, target):
        copy = pltpu.make_async_copy(source, target, self.local_sems.at[self.locals])
        self.locals += 1
        copy.start()
        return copy

    def send(self, source, target, device, when=None):
        place = len(self.remotes)
        copy = pltpu.make_async_remote_copy(
            src_ref=source,
            dst_ref=target,
            send_sem=self.send_sems.at[place],
            recv_sem=self.recv_sems.at[place],
            device_id=device,
            device_id_type=MESH,
        )
        remote = Remote(copy, when)
        remote.start()
        self.remotes.append(remote)
        return remote


class Gather:
    def __init__(self, net, wm, wmv, i, j, lats):
        self.net, self.wmv, self.i = net, wmv, i
        x_hi = j // 8
        y2 = j - x_hi * 8
        self.odd = lax.rem(i // 2, 2)
        across = i + 1 - 2 * lax.rem(i, 2)

        def same(k):
            return x_hi * 8 + lax.rem(y2 + 2 * k + 8, 8)

        def other(k):
            return (1 - x_hi) * 8 + lax.rem(y2 + 2 * k + 8, 8)

        def pick(when_odd, when_even):
            return when_odd * self.odd + when_even * (1 - self.odd)

        self.mate = (i, j + 1 - 2 * lax.rem(j, 2))
        self.z_up, self.z_down = (lax.rem(i + 2, lats), j), (lax.rem(i + lats - 2, lats), j)
        self.targets = [
            (pick(i, across), pick(same(-1), other(-1))),
            (pick(i, across), pick(same(1), other(1))),
            (pick(across, i), pick(other(0), same(2))),
            (across, other(2)),
        ]
        self.mine = [pick(same(1), other(1)), pick(same(-1), other(-1)), pick(other(0), same(2)), other(2)]
        self.theirs = [pick(other(1), same(1)), pick(other(-1), same(-1)), pick(same(2), other(0)), other(2)]
        self.partners = [self.z_up, self.z_down]
        for step in (-1, 1):
            self.partners += [(i, same(step)), (across, other(step))]
        self.partners += [(i, same(2)), (across, other(0)), (across, other(2))]
        self.direct, self.from_z, self.to_mate = {}, {}, []
        self.wm, self.j = wm, j

    def part(self, block, row, rows):
        return self.wmv.at[block, pl.ds(row, rows)]

    def when(self, slot, value):
        return None if slot < 3 else self.odd == value

    def start(self):
        for half in range(2):
            rows = pl.ds(64 * half, 64)
            for slot in range(4):
                self.direct[slot, half] = self.net.send(
                    self.wm.at[rows], self.wmv.at[self.j, rows], self.targets[slot], when=self.when(slot, 1)
                )
        self.to_mate.append(self.net.send(self.wm, self.wmv.at[self.j], self.mate))

    def forward(self, half):
        for slot in (2, 0, 1, 3):
            self.direct[slot, half].wait_recv()
            block, when = self.mine[slot], self.when(slot, 1)
            low, high = self.part(block, 64 * half, 32), self.part(block, 64 * half + 32, 32)
            self.from_z[slot, half] = (
                self.net.send(low, low, self.z_up, when=when),
                self.net.send(high, high, self.z_down, when=when),
            )
            if slot < 3:
                whole = self.part(block, 64 * half, 64)
                self.to_mate.append(self.net.send(whole, whole, self.mate))

    def swapped(self, half):
        for slot in (2, 0, 1, 3):
            for copy in self.from_z[slot, half]:
                copy.wait_recv(self.when(slot, 0))
            whole = self.part(self.theirs[slot], 64 * half, 64)
            self.to_mate.append(self.net.send(whole, whole, self.mate))

    def finish(self):
        for copy in self.to_mate:
            copy.wait_recv()


def body(lats, lons, *refs):
    (tok_in, cot_in, w1i, w1o, wm, w2i, w2o, c0, c1, c1t, c2, c2t, c3, c3t, c4, c4t) = refs[:N_IN]
    out2, outg = refs[N_IN : N_IN + 2]
    rest = refs[N_IN + 2 :]
    v = dict(zip(SCRATCH, rest))
    net = Copies(*rest[len(SCRATCH) :])
    own, tok, fo, lay, g1, gf, tg, wmv = (v[n] for n in ("own", "tok", "fo", "lay", "g1", "gf", "tg", "wmv"))

    i, j = lax.axis_index("lat"), lax.axis_index("lon")
    up, down = lax.rem(i + 1, lats), lax.rem(i + lats - 1, lats)
    right, left = lax.rem(j + 1, lons), lax.rem(j + lons - 1, lons)
    core = lax.rem(j, 2)
    mate = j + 1 - 2 * core
    ring = lons == 16
    partners = [(i, right), (i, left), (up, j), (down, j), (up, right), (down, left)]
    gather = Gather(net, wm, wmv, i, j, lats) if ring else None
    partners += gather.partners if ring else [(i, lax.rem(j + d, lons)) for d in range(1, lons)]

    barrier = pltpu.get_barrier_semaphore()
    for device in partners:
        pl.semaphore_signal(barrier, inc=1, device_id=device, device_id_type=MESH)

    in_raw = net.local(tok_in, v["raw"])
    in_c_raw = net.local(c0, v["c_raw"])
    in_one = net.local(c1, v["one"])
    in_w1i = net.local(w1i, v["w1i_v"])
    in_w1o = net.local(w1o, v["w1o_v"])
    in_one_t = net.local(c1t, v["one_t"])
    in_wm = net.local(wm, wmv.at[j])
    in_rest = [net.local(a, v[n]) for a, n in ((c4, "coa"), (c3, "mer"), (c2, "two"))]
    in_w2i = [
        net.local(
            w2i.at[:, pl.ds(pl.multiple_of(1024 * part + 512 * core, 512), 512)],
            v["w2i_v"].at[:, pl.ds(512 * part, 512)],
        )
        for part in range(3)
    ]
    in_w2o = net.local(w2o, v["w2o_v"])
    in_late = [net.local(a, v[n]) for a, n in ((c2t, "two_t"), (c3t, "mer_t"), (c4t, "coa_t"))]

    in_raw.wait()
    in_c_raw.wait()
    for g in range(4):
        slabs = []
        for lev in range(4):
            for r in range(3):
                slabs += [v["raw"][lev, 3 * g + r].astype(F32), jnp.zeros((4, 512), F32)]
        value = dot(v["c_raw"][...], jnp.concatenate(slabs, axis=0).astype(BF))
        for h in range(2):
            own[h, g] = value[72 * h : 72 * h + 72].astype(BF)

    pl.semaphore_wait(barrier, len(partners))

    r_a = net.send(own.at[0, pl.ds(1, 2)], tok.at[1, pl.ds(0, 2)], (i, left))
    r_b = net.send(own.at[0, pl.ds(3, 1)], tok.at[1, pl.ds(2, 1)], (i, left))
    r_c = net.send(own.at[1, pl.ds(0, 1)], tok.at[0, pl.ds(3, 1)], (down, j))
    r_d = net.send(own.at[0, pl.ds(0, 1)], tok.at[1, pl.ds(3, 1)], (down, left))

    depth = wm.shape[0]
    everywhere = []
    if ring:
        gather.start()
    else:
        for d in range(1, lons):
            everywhere.append(net.send(wm, wmv.at[j], (i, lax.rem(j + d, lons))))

    def merge_rows(b):
        if depth <= 256:
            count = 256 // depth
            return wmv[pl.ds(count * b, count)].reshape(256, 1024)
        return wmv[256 * b // depth, pl.ds(256 * b % depth, 256)]

    cot_a = net.send(cot_in.at[:, pl.ds(3, 3)], v["cot_r"].at[0], (i, left))
    cot_b = net.send(cot_in.at[:, pl.ds(0, 3)], v["cot_r"].at[1], (down, left))

    lane = lax.broadcasted_iota(jnp.int32, (1, 640), 1)
    lane = lane - 160 * (
        (lane >= 160).astype(jnp.int32) + (lane >= 320).astype(jnp.int32) + (lane >= 480).astype(jnp.int32)
    )
    key = lax.broadcasted_iota(jnp.int32, (144, 1), 0)

    def quarter(index):
        return (index >= 36).astype(jnp.int32) + (index >= 72).astype(jnp.int32) + (index >= 108).astype(jnp.int32)

    pad = lane >= 144
    half_mask = jnp.where(((key >= 72) == (lane >= 72)) | pad, 0.0, -1e30)
    quarter_mask = jnp.where((quarter(key) == quarter(lane)) | pad, 0.0, -1e30)
    last = jnp.broadcast_to(i, (144, 640)) == lats - 1
    v["mk"][0, 0] = jnp.zeros((144, 640), F32)
    v["mk"][0, 1] = half_mask
    v["mk"][1, 0] = jnp.where(last, half_mask, 0.0)
    v["mk"][1, 1] = jnp.where(last, quarter_mask, half_mask)

    def rows_of(parts):
        return jnp.concatenate([part.astype(F32) for part in parts], axis=0)

    def rolled(h, g):
        return own[1, g + 1] if h == 0 and g < 3 else tok[h, g]

    def rolled_tokens(w):
        return rows_of([rolled(h, 2 * w + g) for h in range(2) for g in range(2)])

    def put_pieces(ref, w, value):
        for k in range(4):
            ref[k // 2, 2 * w + k % 2] = value[72 * k : 72 * k + 72].astype(BF)

    def section_one(w):
        x = rolled_tokens(w)
        hat, scale = norm(x)
        normed = hat.astype(BF)
        v["nrm"][w] = normed
        v["rs1"][w] = jnp.broadcast_to(scale, (288, 128))
        blocks = dot(v["one"][...], normed).astype(BF)
        for n in range(0, 1536, 256):
            v["trip1"][w, :, pl.ds(n, 256)] = dot(blocks, v["w1i_v"][:, pl.ds(n, 256)]).astype(BF)
        attend(v["trip1"].at[w], v["mk"].at[w], v["mix"], v["ps1"].at[w])
        projected = dot(v["mix"][...], v["w1o_v"][...]).astype(BF)
        put_pieces(fo, w, rolled_tokens(w) + dot(v["one_t"][...], projected))

    in_one.wait()
    in_w1i.wait()
    in_w1o.wait()
    in_one_t.wait()
    r_a.wait_recv()
    section_one(0)
    f_a = net.send(fo.at[0, pl.ds(1, 1)], lay.at[1, pl.ds(0, 1)], (i, left))
    f_b = net.send(fo.at[0, pl.ds(0, 1)], lay.at[1, pl.ds(3, 1)], (down, left))
    f_c = net.send(fo.at[1, pl.ds(0, 1)], lay.at[0, pl.ds(3, 1)], (down, j))
    if ring:
        gather.forward(0)
    r_b.wait_recv()
    r_c.wait_recv()
    r_d.wait_recv()
    section_one(1)
    f_d = net.send(fo.at[0, pl.ds(2, 2)], lay.at[1, pl.ds(1, 2)], (i, left))

    for copy in in_rest:
        copy.wait()
    cot_a.wait_recv()
    cot_b.wait_recv()
    slabs = []
    for slab in range(24):
        slabs += [v["cot_r"][slab // 12, slab // 3 % 4, slab % 3].astype(F32), jnp.zeros((2, 1024), F32)]
    v["cot2"][0] = dot(v["coa"][...], jnp.concatenate(slabs, axis=0).astype(BF)).astype(BF)
    cot_m = net.send(v["cot2"].at[0], v["cot2"].at[1], (i, mate))

    if ring:
        gather.forward(1)

    def merge_half(h, parts):
        value = dot(v["mer"][...], rows_of(parts).astype(BF))
        for pq in range(4):
            v["mf"][pl.ds(72 * h, 72), pl.ds(512 * pq, 512)] = value[72 * pq : 72 * pq + 72]

    f_c.wait_recv()
    merge_half(0, [fo[1, 1], fo[1, 2], fo[1, 3], lay[0, 3]])
    f_a.wait_recv()
    f_b.wait_recv()
    f_d.wait_recv()
    merge_half(1, [lay[1, g] for g in range(4)])
    if ring:
        gather.swapped(0)
    hat, scale = norm(v["mf"][...])
    v["mn"][...] = hat.astype(BF)
    v["rsm"][...] = jnp.broadcast_to(scale, (144, 128))
    in_wm.wait()
    if ring:
        gather.swapped(1)
        gather.finish()
    for copy in everywhere:
        copy.wait_recv()
    merged = v["mn"][...]
    for n in range(0, 1024, 256):
        v["red"][:, pl.ds(n, 256)] = dot(merged, wmv[:, :, pl.ds(n, 256)].reshape(2048, 256)).astype(BF)
    hat, scale = norm(v["red"][...].astype(F32))
    v["nt"][0] = hat.astype(BF)
    v["rs2"][...] = jnp.broadcast_to(scale, (144, 128))
    n_m = net.send(v["nt"].at[0], v["nt"].at[1], (i, mate))

    own_rows = pl.ds(pl.multiple_of(512 * core, 512), 512)
    far_rows = pl.ds(pl.multiple_of(512 - 512 * core, 512), 512)
    in_w2o.wait()
    cot_m.wait_recv()
    grad_blocks = dot(v["two"][...], v["cot2"][...].reshape(288, 1024)).astype(BF)
    v["dmix2"][...] = dot(grad_blocks, v["w2o_v"][own_rows, :], NT).astype(BF)
    for copy in in_w2i + in_late:
        copy.wait()
    n_m.wait_recv()

    blocks = dot(v["two"][...], v["nt"][...].reshape(288, 1024)).astype(BF)
    for n in range(0, 1536, 256):
        v["trip2"][:, pl.ds(n, 256)] = dot(blocks, v["w2i_v"][:, pl.ds(n, 256)]).astype(BF)
    attend(v["trip2"], v["mk"].at[1], v["mix2"], v["ps2"])
    mixed = dot(v["two_t"][...], v["mix2"][...]).astype(BF)
    v["mxo"][...] = mixed[:144]
    v["mxs"][...] = mixed[144:]
    x_m = net.send(v["mxs"], v["mxr"], (i, mate))

    attend_back(v["trip2"], v["dmix2"], v["ps2"], v["dtrip"])
    back = dot(v["two_t"][...], v["dtrip"][...]).astype(BF)
    for n in range(0, 1024, 256):
        v["pgs"][:, pl.ds(n, 256)] = dot(back[144:], v["w2i_v"][pl.ds(n, 256), :], NT).astype(BF)
    p_m = net.send(v["pgs"], v["pgr"], (i, mate))
    for n in range(0, 1024, 256):
        v["pgo"][:, pl.ds(n, 256)] = dot(back[:144], v["w2i_v"][pl.ds(n, 256), :], NT)
    p_m.wait_recv()
    grad = (v["pgo"][...] + v["pgr"][...].astype(F32)).astype(BF).astype(F32)
    grad = norm_back(grad, v["nt"][0].astype(F32), v["rs2"][:, :1])
    v["gr"][...] = (grad + v["cot2"][0].astype(F32)).astype(BF)
    for b in range(8):
        rows = merge_rows(b)
        v["gmn"][:, pl.ds(256 * b, 256)] = dot(v["gr"][...], rows, NT).astype(BF)
    v["mf"][...] = norm_back(v["gmn"][...].astype(F32), v["mn"][...].astype(F32), v["rsm"][:, :1])

    def unmerge_half(h):
        rows = v["mf"][pl.ds(72 * h, 72), :]
        value = jnp.concatenate([rows[:, 512 * pq : 512 * pq + 512] for pq in range(4)], axis=0).astype(BF)
        value = dot(v["mer_t"][...], value)
        return [value[72 * g : 72 * g + 72].astype(BF) for g in range(4)]

    for g, value in enumerate(unmerge_half(1)):
        gf[1, g] = value
    b_a = net.send(gf.at[1, pl.ds(1, 2)], g1.at[0, pl.ds(2, 2)], (i, right))
    b_b = net.send(gf.at[1, pl.ds(0, 1)], g1.at[0, pl.ds(1, 1)], (i, right))
    b_c = net.send(gf.at[1, pl.ds(3, 1)], g1.at[0, pl.ds(0, 1)], (up, right))
    parts = unmerge_half(0)
    gf[0, 3] = parts[3]
    b_d = net.send(gf.at[0, pl.ds(3, 1)], g1.at[1, pl.ds(0, 1)], (up, j))
    for g in range(3):
        g1[1, g + 1] = parts[g]

    x_m.wait_recv()
    attended = dot(v["mxo"][...], v["w2o_v"][own_rows, :]) + dot(v["mxr"][...], v["w2o_v"][far_rows, :])
    result = (v["red"][...].astype(F32) + attended.astype(BF).astype(F32)).astype(BF)
    slabs = dot(v["coa_t"][...], result)
    for slab in range(24):
        v["s2o"][slab // 12, slab // 3 % 4, slab % 3] = slabs[8 * slab : 8 * slab + 6].astype(BF)
    o_a = net.send(v["s2o"].at[0], out2.at[:, pl.ds(3, 3)], (i, right))
    o_b = net.send(v["s2o"].at[1], out2.at[:, pl.ds(0, 3)], (up, right))

    def section_one_back(w):
        arrived = rows_of([g1[h, 2 * w + g] for h in range(2) for g in range(2)])
        grad_blocks = dot(v["one"][...], arrived.astype(BF)).astype(BF)
        v["dmix"][...] = dot(grad_blocks, v["w1o_v"][...], NT).astype(BF)
        attend_back(v["trip1"].at[w], v["dmix"], v["ps1"].at[w], v["dtrip"])
        grad = dot(v["dtrip"][...], v["w1i_v"][...], NT).astype(BF)
        grad = dot(v["one_t"][...], grad)
        grad = norm_back(grad, v["nrm"][w].astype(F32), v["rs1"][w, :, :1])
        put_pieces(tg, w, grad + rows_of([g1[h, 2 * w + g] for h in range(2) for g in range(2)]))

    b_a.wait_recv()
    section_one_back(1)
    t_a = net.send(tg.at[1, pl.ds(2, 1)], outg.at[0, pl.ds(3, 1)], (i, right))
    t_b = net.send(tg.at[1, pl.ds(3, 1)], outg.at[0, pl.ds(0, 1)], (up, right))
    t_c = net.send(tg.at[0, pl.ds(3, 1)], outg.at[1, pl.ds(0, 1)], (up, j))
    keep_a = net.local(tg.at[0, pl.ds(2, 1)], outg.at[1, pl.ds(3, 1)])
    b_b.wait_recv()
    b_c.wait_recv()
    b_d.wait_recv()
    section_one_back(0)
    t_d = net.send(tg.at[1, pl.ds(0, 2)], outg.at[0, pl.ds(1, 2)], (i, right))
    keep_b = net.local(tg.at[0, pl.ds(0, 2)], outg.at[1, pl.ds(1, 2)])
    for copy in (o_a, o_b, t_a, t_b, t_c, t_d):
        copy.wait_recv()
    keep_a.wait()
    keep_b.wait()
    for copy in net.remotes:
        copy.wait_send()


def local(tokens, cotangent, *weights, lats, lons):
    shapes = dict(SCRATCH, wmv=((lons, 2048 // lons, 1024), BF))
    constants = [jnp.asarray(a) for a in orders()]
    anywhere = pl.BlockSpec(memory_space=pl.ANY)
    out2, outg = pl.pallas_call(
        functools.partial(body, lats, lons),
        out_shape=(jax.ShapeDtypeStruct((4, 6, 6, 1024), BF), jax.ShapeDtypeStruct((2, 4, 72, 512), BF)),
        in_specs=[anywhere] * N_IN,
        out_specs=(anywhere, anywhere),
        scratch_shapes=[pltpu.VMEM(shape, kind) for shape, kind in shapes.values()]
        + [pltpu.SemaphoreType.DMA((24,)), pltpu.SemaphoreType.DMA((N_SEM,)), pltpu.SemaphoreType.DMA((N_SEM,))],
        compiler_params=pltpu.CompilerParams(
            collective_id=0, has_side_effects=True, vmem_limit_bytes=56 * 2**20
        ),
        name="swin",
    )(tokens, cotangent, *weights, *constants)
    grad = outg.reshape(2, 4, 4, 3, 6, 512).transpose(2, 1, 3, 0, 4, 5).reshape(4, 12, 12, 512)
    return out2, grad


def solution(mesh):
    tiles = P(None, "lat", "lon", None)
    return jax.shard_map(
        functools.partial(local, lats=mesh.shape["lat"], lons=mesh.shape["lon"]),
        mesh=mesh,
        in_specs=(tiles, tiles, P(), P(), P("lon", None), P(), P()),
        out_specs=(tiles, tiles),
        check_vma=False,
    )
```

time: 302 us -> 80.1 us (0.27); the launches traced: 296 us -> 79.8 us
  waiting for transfers between devices: 78 us -> 0 us
  Pallas kernels: 0 us -> 70.8 us
  local copies, waits for them, and re-layouts: 77.8 us -> 8.34 us
  matrix products: 64.2 us -> 0 us
  other arithmetic: 36.9 us -> 0 us
  starting transfers between devices: 24 us -> 0 us
  between operations: 15.4 us -> 0.64 us
    ppermute x18 -> x0, waiting for transfers between devices: 77.4 us -> none  [the longest x16 77.4 us: from_behind(): return lax.ppermute(value, axis, pairs)]
    pallas_call x0 -> x1, Pallas kernels: none -> 70.8 us  [local(): pl.pallas_call(functools.partial(body, lats, lons), out_shape=(jax.ShapeD...]
    dot_general x22 -> x0, matrix products: 64.2 us -> none  [the longest x6 20.4 us: attend(): jnp.einsum('nqhd,nkhd->nhqk', query_heads, key_heads) * head_size ** (-0.5)]
    ppermute x18 -> x0, starting transfers between devices: 24 us -> none  [the longest x16 23.2 us: from_behind(): return lax.ppermute(value, axis, pairs)]
    reshape x17 -> x0, local copies, waits for them, and re-layouts: 21.2 us -> none  [the longest x2 3.89 us: attend(): return blended.reshape(number, query_len, channels).astype(jnp.bfloat16)]
    slice x35 -> x0, local copies, waits for them, and re-layouts: 20.1 us -> none  [the longest x20 3.83 us: move_rows(): grid_field = jnp.roll(grid_field, -direction, axis=0)]
    convert_element_type x12 -> x0, local copies, waits for them, and re-layouts: 18.4 us -> none  [the longest x4 8.61 us: attend(): return blended.reshape(number, query_len, channels).astype(jnp.bfloat16)]
    concatenate x17 -> x0, other arithmetic: 14.5 us -> none  [the longest x10 7.91 us: move_rows(): jnp.concatenate([remain, arrived] if direction == 1 else [arrived, remain...]
  transfers between devices with their start and end apart: 19 -> 0, of which waited for: 14 -> 0; matrix products, arithmetic and copies ran while one was open for 30% -> 0% of each run, Pallas kernels for 0% -> 0%
where the time goes in v1:
time: 80.1 us; the launch traced here: 79.8 us
  Pallas kernels  70.8 us (88%)
  local copies, waits for them, and re-layouts  8.34 us (10%)
    pallas_call x1, Pallas kernels, local(): pl.pallas_call(functools.partial(body, lats, lons), out_shape=(jax.ShapeD...  70.8 us
    unnamed x3, local copies, waits for them, and re-layouts  5.86 us

profile of v1, /device:TPU:2, one launch (start us, length us, event | category | flops | bytes accessed | tf_op | source)
XLA Modules:
  0.0 79.8 jit_solution(2313612580641290064)
XLA Ops:
  0.6 1.8 %copy.27.refs_1_ = bf16[4,6,6,1024]{3,2,1,0:T(8,128)(2,1)} copy(bf16[4,6,6,1024]{3,0,2,1:T(4,128)(2,1)} %param.17) | data formatting | bytes 589824 | tf_op args[1]
  2.4 2.1 %copy.26.refs_0_ = bf16[4,12,12,512]{3,2,1,0:T(8,128)(2,1)} copy(bf16[4,12,12,512]{3,0,2,1:T(4,128)(2,1)} %param.16) | data formatting | bytes 1179648 | tf_op args[0]
  4.5 70.8 %swin.1 = (bf16[4,6,6,1024]{3,2,1,0:T(8,128)(2,1)}, bf16[2,4,72,512]{3,2,1,0:T(8,128)(2,1)}) custom-call(bf16[4,12,12,512]{3,2,1,0:T(8,128)(2,1)} %copy.26.refs_0_, bf16[4,6,6,1024]{3,2,1,0:T(8,128)(2,1)} %copy.27.refs_1_, bf16[512,1536]{1,0:T(8,128)(2,1)} %refs_2_.1, bf16[512,512]{1,0:T(8,128)(2,1)} %refs_3_.1, bf16[128,1024]{1,0:T(8,128)(2,1)} %refs_4_.1, ...), custom_call_target="tpu_custom_call" | custom-call | tf_op jit(solution)/shard_map/swin/pallas_call | solution.py:590
  75.4 1.9 %copy.30 = bf16[4,6,6,1024]{3,0,2,1:T(4,128)(2,1)} copy(bf16[4,6,6,1024]{3,2,1,0:T(8,128)(2,1)} %get-tuple-element.10) | data formatting | bytes 589824
  77.3 1.4 %copy.28 = bf16[2,4,72,512]{3,1,2,0:T(4,128)(2,1)S(1)} copy(bf16[2,4,72,512]{3,2,1,0:T(8,128)(2,1)} %get-tuple-element.5) | data formatting | bytes 1179648 | tf_op jit(solution)/shard_map/swin/pallas_call | solution.py:590
  78.7 1.1 %copy.29 = bf16[4,4,3,2,6,512]{5,0,4,3,2,1:T(4,128)(2,1)} copy(bf16[4,4,3,2,6,512]{5,1,4,2,0,3:T(4,128)(2,1)S(1)} %bitcast.4) | data formatting | bytes 1179648 | tf_op jit(solution)/shard_map/transpose | solution.py:602

commit v2 on v1

--- a/solution.py
+++ b/solution.py
@@ -30,44 +30,29 @@
 
 @functools.lru_cache(None)
 def orders():
-    raw = np.zeros((144, 192), np.float32)
-    for h in range(2):
-        for slab in range(12):
-            for k in range(6):
-                raw[h * 72 + slab * 6 + k, slab * 16 + 6 * h + k] = 1
     one = np.zeros((288, 288), np.float32)
     counters = {}
-    for h in range(2):
-        for g in range(2):
+    for row in range(6):
+        for col in range(12):
             for lev in range(4):
-                for k in range(18):
-                    one[window_place(lev, g, counters), (h * 2 + g) * 72 + lev * 18 + k] = 1
+                one[window_place(lev, row // 3, counters), row * 48 + col * 4 + lev] = 1
     two = np.zeros((288, 288), np.float32)
     counters = {}
     for m in range(2):
         for h in range(2):
-            for lev in range(4):
-                for i in range(6):
-                    for j in range(3):
-                        two[window_place(lev, i // 3, counters), m * 144 + h * 72 + lev * 18 + i * 3 + j] = 1
+            for row in range(6):
+                for col in range(3):
+                    for lev in range(4):
+                        two[window_place(lev, row // 3, counters), m * 144 + h * 72 + row * 12 + col * 4 + lev] = 1
     merge = np.zeros((288, 288), np.float32)
     for p in range(2):
         for q in range(2):
-            for lev in range(4):
-                for i in range(6):
-                    for j in range(3):
-                        row, col = 2 * i + p, 2 * j + q
-                        source = (row // 3) * 72 + lev * 18 + (row % 3) * 6 + col
-                        merge[(p * 2 + q) * 72 + lev * 18 + i * 3 + j, source] = 1
-    coarse = np.zeros((144, 192), np.float32)
-    for h in range(2):
-        for lev in range(4):
-            for i in range(6):
-                for j in range(3):
-                    slab = ((i // 3) * 4 + lev) * 3 + i % 3
-                    coarse[h * 72 + lev * 18 + i * 3 + j, slab * 8 + h * 3 + j] = 1
-    mats = (raw, one, one.T, two, two.T, merge, merge.T, coarse, coarse.T)
-    return tuple(np.asarray(m, dtype=BF) for m in mats)
+            for row in range(6):
+                for col in range(3):
+                    for lev in range(4):
+                        source = (2 * row + p) * 24 + (2 * col + q) * 4 + lev
+                        merge[(p * 2 + q) * 72 + row * 12 + col * 4 + lev, source] = 1
+    return tuple(np.asarray(m, dtype=BF) for m in (one, one.T, two, two.T, merge, merge.T))
 
 
 def head_rows():
@@ -136,17 +121,15 @@
 
 
 SCRATCH = dict(
-    raw=((4, 12, 12, 512), BF),
-    own=((2, 4, 72, 512), BF),
-    tok=((2, 4, 72, 512), BF),
+    tk=((12, 12, 4, 512), BF),
     nrm=((2, 288, 512), BF),
     rs1=((2, 288, 128), F32),
     trip1=((2, 288, 1536), BF),
     ps1=((2, 4, 144, 640), BF),
     mix=((288, 512), BF),
     mk=((2, 2, 144, 640), F32),
-    fo=((2, 4, 72, 512), BF),
-    lay=((2, 4, 72, 512), BF),
+    fo=((12, 12, 4, 512), BF),
+    ly=((12, 12, 4, 512), BF),
     mf=((144, 2048), F32),
     mn=((144, 2048), BF),
     rsm=((144, 128), F32),
@@ -158,16 +141,13 @@
     wmv=((16, 128, 1024), BF),
     w2i_v=((1024, 1536), BF),
     w2o_v=((1024, 1024), BF),
-    c_raw=((144, 192), BF),
     one=((288, 288), BF),
     one_t=((288, 288), BF),
     two=((288, 288), BF),
     two_t=((288, 288), BF),
     mer=((288, 288), BF),
     mer_t=((288, 288), BF),
-    coa=((144, 192), BF),
-    coa_t=((192, 144), BF),
-    cot_r=((2, 4, 3, 6, 1024), BF),
+    cot_r=((6, 6, 4, 1024), BF),
     cot2=((2, 144, 1024), BF),
     trip2=((288, 1536), BF),
     ps2=((4, 144, 640), BF),
@@ -183,12 +163,12 @@
     pgo=((144, 1024), F32),
     gr=((144, 1024), BF),
     gmn=((144, 2048), BF),
-    gf=((2, 4, 72, 512), BF),
-    g1=((2, 4, 72, 512), BF),
-    tg=((2, 4, 72, 512), BF),
-    s2o=((2, 4, 3, 6, 1024), BF),
+    gf=((12, 12, 4, 512), BF),
+    g1=((12, 12, 4, 512), BF),
+    tg=((12, 12, 4, 512), BF),
+    s2o=((6, 6, 4, 1024), BF),
 )
-N_IN = 16
+N_IN = 13
 N_SEM = 80
 
 
@@ -258,18 +238,17 @@
 
         self.mate = (i, j + 1 - 2 * lax.rem(j, 2))
         self.z_up, self.z_down = (lax.rem(i + 2, lats), j), (lax.rem(i + lats - 2, lats), j)
-        self.targets = [
-            (pick(i, across), pick(same(-1), other(-1))),
-            (pick(i, across), pick(same(1), other(1))),
-            (pick(across, i), pick(other(0), same(2))),
-            (across, other(2)),
-        ]
-        self.mine = [pick(same(1), other(1)), pick(same(-1), other(-1)), pick(other(0), same(2)), other(2)]
-        self.theirs = [pick(other(1), same(1)), pick(other(-1), same(-1)), pick(same(2), other(0)), other(2)]
-        self.partners = [self.z_up, self.z_down]
+        self.targets = {
+            0: (pick(i, across), pick(same(-1), other(-1))),
+            1: (pick(i, across), pick(same(1), other(1))),
+            3: (across, other(0)),
+        }
+        self.onward = (i, same(1))
+        self.mine = [pick(same(1), other(1)), pick(same(-1), other(-1)), pick(same(2), other(2)), other(0)]
+        self.theirs = [pick(other(1), same(1)), pick(other(-1), same(-1)), pick(other(2), same(2)), other(0)]
+        self.partners = [self.z_up, self.z_down, (across, other(0))]
         for step in (-1, 1):
             self.partners += [(i, same(step)), (across, other(step))]
-        self.partners += [(i, same(2)), (across, other(0)), (across, other(2))]
         self.direct, self.from_z, self.to_mate = {}, {}, []
         self.wm, self.j = wm, j
 
@@ -282,31 +261,31 @@
     def start(self):
         for half in range(2):
             rows = pl.ds(64 * half, 64)
-            for slot in range(4):
+            for slot in (1, 3, 0):
                 self.direct[slot, half] = self.net.send(
                     self.wm.at[rows], self.wmv.at[self.j, rows], self.targets[slot], when=self.when(slot, 1)
                 )
         self.to_mate.append(self.net.send(self.wm, self.wmv.at[self.j], self.mate))
 
-    def forward(self, half):
-        for slot in (2, 0, 1, 3):
-            self.direct[slot, half].wait_recv()
-            block, when = self.mine[slot], self.when(slot, 1)
-            low, high = self.part(block, 64 * half, 32), self.part(block, 64 * half + 32, 32)
-            self.from_z[slot, half] = (
-                self.net.send(low, low, self.z_up, when=when),
-                self.net.send(high, high, self.z_down, when=when),
-            )
-            if slot < 3:
-                whole = self.part(block, 64 * half, 64)
-                self.to_mate.append(self.net.send(whole, whole, self.mate))
-
-    def swapped(self, half):
-        for slot in (2, 0, 1, 3):
-            for copy in self.from_z[slot, half]:
-                copy.wait_recv(self.when(slot, 0))
-            whole = self.part(self.theirs[slot], 64 * half, 64)
+    def forward(self, slot, half):
+        self.direct[slot, half].wait_recv()
+        block, when = self.mine[slot], self.when(slot, 1)
+        whole = self.part(block, 64 * half, 64)
+        if slot == 1:
+            self.direct[2, half] = self.net.send(whole, whole, self.onward)
+        low, high = self.part(block, 64 * half, 32), self.part(block, 64 * half + 32, 32)
+        self.from_z[slot, half] = (
+            self.net.send(low, low, self.z_up, when=when),
+            self.net.send(high, high, self.z_down, when=when),
+        )
+        if slot < 3:
             self.to_mate.append(self.net.send(whole, whole, self.mate))
+
+    def swapped(self, slot, half):
+        for copy in self.from_z[slot, half]:
+            copy.wait_recv(self.when(slot, 0))
+        whole = self.part(self.theirs[slot], 64 * half, 64)
+        self.to_mate.append(self.net.send(whole, whole, self.mate))
 
     def finish(self):
         for copy in self.to_mate:
@@ -314,12 +293,12 @@
 
 
 def body(lats, lons, *refs):
-    (tok_in, cot_in, w1i, w1o, wm, w2i, w2o, c0, c1, c1t, c2, c2t, c3, c3t, c4, c4t) = refs[:N_IN]
+    (tok_in, cot_in, w1i, w1o, wm, w2i, w2o, c1, c1t, c2, c2t, c3, c3t) = refs[:N_IN]
     out2, outg = refs[N_IN : N_IN + 2]
     rest = refs[N_IN + 2 :]
     v = dict(zip(SCRATCH, rest))
     net = Copies(*rest[len(SCRATCH) :])
-    own, tok, fo, lay, g1, gf, tg, wmv = (v[n] for n in ("own", "tok", "fo", "lay", "g1", "gf", "tg", "wmv"))
+    tk, fo, ly, g1, gf, tg, wmv = (v[n] for n in ("tk", "fo", "ly", "g1", "gf", "tg", "wmv"))
 
     i, j = lax.axis_index("lat"), lax.axis_index("lon")
     up, down = lax.rem(i + 1, lats), lax.rem(i + lats - 1, lats)
@@ -335,14 +314,14 @@
     for device in partners:
         pl.semaphore_signal(barrier, inc=1, device_id=device, device_id_type=MESH)
 
-    in_raw = net.local(tok_in, v["raw"])
-    in_c_raw = net.local(c0, v["c_raw"])
+    first, later, near, far = pl.ds(0, 3), pl.ds(3, 9), pl.ds(0, 6), pl.ds(6, 6)
+    in_tok = net.local(tok_in.at[later, far], tk.at[pl.ds(0, 9), near])
     in_one = net.local(c1, v["one"])
     in_w1i = net.local(w1i, v["w1i_v"])
     in_w1o = net.local(w1o, v["w1o_v"])
     in_one_t = net.local(c1t, v["one_t"])
     in_wm = net.local(wm, wmv.at[j])
-    in_rest = [net.local(a, v[n]) for a, n in ((c4, "coa"), (c3, "mer"), (c2, "two"))]
+    in_rest = [net.local(a, v[n]) for a, n in ((c3, "mer"), (c2, "two"))]
     in_w2i = [
         net.local(
             w2i.at[:, pl.ds(pl.multiple_of(1024 * part + 512 * core, 512), 512)],
@@ -351,25 +330,14 @@
         for part in range(3)
     ]
     in_w2o = net.local(w2o, v["w2o_v"])
-    in_late = [net.local(a, v[n]) for a, n in ((c2t, "two_t"), (c3t, "mer_t"), (c4t, "coa_t"))]
-
-    in_raw.wait()
-    in_c_raw.wait()
-    for g in range(4):
-        slabs = []
-        for lev in range(4):
-            for r in range(3):
-                slabs += [v["raw"][lev, 3 * g + r].astype(F32), jnp.zeros((4, 512), F32)]
-        value = dot(v["c_raw"][...], jnp.concatenate(slabs, axis=0).astype(BF))
-        for h in range(2):
-            own[h, g] = value[72 * h : 72 * h + 72].astype(BF)
+    in_late = [net.local(a, v[n]) for a, n in ((c2t, "two_t"), (c3t, "mer_t"))]
 
     pl.semaphore_wait(barrier, len(partners))
 
-    r_a = net.send(own.at[0, pl.ds(1, 2)], tok.at[1, pl.ds(0, 2)], (i, left))
-    r_b = net.send(own.at[0, pl.ds(3, 1)], tok.at[1, pl.ds(2, 1)], (i, left))
-    r_c = net.send(own.at[1, pl.ds(0, 1)], tok.at[0, pl.ds(3, 1)], (down, j))
-    r_d = net.send(own.at[0, pl.ds(0, 1)], tok.at[1, pl.ds(3, 1)], (down, left))
+    r_a = net.send(tok_in.at[pl.ds(3, 6), near], tk.at[pl.ds(0, 6), far], (i, left))
+    r_b = net.send(tok_in.at[pl.ds(9, 3), near], tk.at[pl.ds(6, 3), far], (i, left))
+    r_c = net.send(tok_in.at[first, far], tk.at[pl.ds(9, 3), near], (down, j))
+    r_d = net.send(tok_in.at[first, near], tk.at[pl.ds(9, 3), far], (down, left))
 
     depth = wm.shape[0]
     everywhere = []
@@ -384,9 +352,6 @@
             count = 256 // depth
             return wmv[pl.ds(count * b, count)].reshape(256, 1024)
         return wmv[256 * b // depth, pl.ds(256 * b % depth, 256)]
-
-    cot_a = net.send(cot_in.at[:, pl.ds(3, 3)], v["cot_r"].at[0], (i, left))
-    cot_b = net.send(cot_in.at[:, pl.ds(0, 3)], v["cot_r"].at[1], (down, left))
 
     lane = lax.broadcasted_iota(jnp.int32, (1, 640), 1)
     lane = lane - 160 * (
@@ -406,81 +371,77 @@
     v["mk"][1, 0] = jnp.where(last, half_mask, 0.0)
     v["mk"][1, 1] = jnp.where(last, quarter_mask, half_mask)
 
-    def rows_of(parts):
-        return jnp.concatenate([part.astype(F32) for part in parts], axis=0)
-
-    def rolled(h, g):
-        return own[1, g + 1] if h == 0 and g < 3 else tok[h, g]
-
-    def rolled_tokens(w):
-        return rows_of([rolled(h, 2 * w + g) for h in range(2) for g in range(2)])
-
-    def put_pieces(ref, w, value):
-        for k in range(4):
-            ref[k // 2, 2 * w + k % 2] = value[72 * k : 72 * k + 72].astype(BF)
-
-    def section_one(w):
-        x = rolled_tokens(w)
-        hat, scale = norm(x)
+    def window_rows(ref, w):
+        return ref[pl.ds(6 * w, 6)].astype(F32).reshape(288, 512)
+
+    def section_one(w, between):
+        hat, scale = norm(window_rows(tk, w))
         normed = hat.astype(BF)
         v["nrm"][w] = normed
         v["rs1"][w] = jnp.broadcast_to(scale, (288, 128))
         blocks = dot(v["one"][...], normed).astype(BF)
         for n in range(0, 1536, 256):
             v["trip1"][w, :, pl.ds(n, 256)] = dot(blocks, v["w1i_v"][:, pl.ds(n, 256)]).astype(BF)
+        pump(between)
         attend(v["trip1"].at[w], v["mk"].at[w], v["mix"], v["ps1"].at[w])
         projected = dot(v["mix"][...], v["w1o_v"][...]).astype(BF)
-        put_pieces(fo, w, rolled_tokens(w) + dot(v["one_t"][...], projected))
+        value = window_rows(tk, w) + dot(v["one_t"][...], projected)
+        fo[pl.ds(6 * w, 6)] = value.reshape(6, 12, 4, 512).astype(BF)
+
+    def pump(steps):
+        if ring:
+            for act, slot, half in steps:
+                getattr(gather, act)(slot, half)
 
     in_one.wait()
     in_w1i.wait()
     in_w1o.wait()
     in_one_t.wait()
+    in_tok.wait()
     r_a.wait_recv()
-    section_one(0)
-    f_a = net.send(fo.at[0, pl.ds(1, 1)], lay.at[1, pl.ds(0, 1)], (i, left))
-    f_b = net.send(fo.at[0, pl.ds(0, 1)], lay.at[1, pl.ds(3, 1)], (down, left))
-    f_c = net.send(fo.at[1, pl.ds(0, 1)], lay.at[0, pl.ds(3, 1)], (down, j))
-    if ring:
-        gather.forward(0)
+    pump([("forward", 1, 0)])
+    section_one(0, [("forward", 3, 0)])
+    f_a = net.send(fo.at[pl.ds(3, 3), near], ly.at[pl.ds(0, 3), far], (i, left))
+    f_b = net.send(fo.at[first, near], ly.at[pl.ds(9, 3), far], (down, left))
+    f_c = net.send(fo.at[first, far], ly.at[pl.ds(9, 3), near], (down, j))
+    pump([("forward", 0, 0), ("forward", 1, 1)])
     r_b.wait_recv()
     r_c.wait_recv()
     r_d.wait_recv()
-    section_one(1)
-    f_d = net.send(fo.at[0, pl.ds(2, 2)], lay.at[1, pl.ds(1, 2)], (i, left))
-
+    section_one(1, [("forward", 2, 0), ("forward", 3, 1)])
+    f_d = net.send(fo.at[pl.ds(6, 6), near], ly.at[pl.ds(3, 6), far], (i, left))
+    ly[pl.ds(0, 9), near] = fo[later, far]
+    pump([("forward", 0, 1), ("swapped", 1, 0), ("swapped", 3, 0), ("swapped", 0, 0), ("forward", 2, 1)])
+    cot_a = net.send(cot_in.at[pl.ds(3, 3)], v["cot_r"].at[pl.ds(0, 3)], (i, left))
+    cot_b = net.send(cot_in.at[pl.ds(0, 3)], v["cot_r"].at[pl.ds(3, 3)], (down, left))
     for copy in in_rest:
         copy.wait()
-    cot_a.wait_recv()
-    cot_b.wait_recv()
-    slabs = []
-    for slab in range(24):
-        slabs += [v["cot_r"][slab // 12, slab // 3 % 4, slab % 3].astype(F32), jnp.zeros((2, 1024), F32)]
-    v["cot2"][0] = dot(v["coa"][...], jnp.concatenate(slabs, axis=0).astype(BF)).astype(BF)
-    cot_m = net.send(v["cot2"].at[0], v["cot2"].at[1], (i, mate))
-
-    if ring:
-        gather.forward(1)
-
-    def merge_half(h, parts):
-        value = dot(v["mer"][...], rows_of(parts).astype(BF))
+
+    def merge_half(h):
+        value = dot(v["mer"][...], ly[:, pl.ds(6 * h, 6)].astype(F32).reshape(288, 512).astype(BF))
         for pq in range(4):
             v["mf"][pl.ds(72 * h, 72), pl.ds(512 * pq, 512)] = value[72 * pq : 72 * pq + 72]
 
     f_c.wait_recv()
-    merge_half(0, [fo[1, 1], fo[1, 2], fo[1, 3], lay[0, 3]])
+    merge_half(0)
     f_a.wait_recv()
     f_b.wait_recv()
     f_d.wait_recv()
-    merge_half(1, [lay[1, g] for g in range(4)])
-    if ring:
-        gather.swapped(0)
+    merge_half(1)
+    pump([("swapped", 2, 0), ("swapped", 1, 1), ("swapped", 3, 1), ("swapped", 0, 1)])
     hat, scale = norm(v["mf"][...])
     v["mn"][...] = hat.astype(BF)
     v["rsm"][...] = jnp.broadcast_to(scale, (144, 128))
+    pump([("swapped", 2, 1)])
+
+    cot_a.wait_recv()
+    cot_b.wait_recv()
+    halves = [v["cot_r"][:, pl.ds(3 * h, 3)].astype(F32).reshape(72, 1024) for h in range(2)]
+    v["cot2"][0] = jnp.concatenate(halves, axis=0).astype(BF)
+    cot_m = net.send(v["cot2"].at[0], v["cot2"].at[1], (i, mate))
+
     in_wm.wait()
     if ring:
-        gather.swapped(1)
         gather.finish()
     for copy in everywhere:
         copy.wait_recv()
@@ -530,51 +491,46 @@
     def unmerge_half(h):
         rows = v["mf"][pl.ds(72 * h, 72), :]
         value = jnp.concatenate([rows[:, 512 * pq : 512 * pq + 512] for pq in range(4)], axis=0).astype(BF)
-        value = dot(v["mer_t"][...], value)
-        return [value[72 * g : 72 * g + 72].astype(BF) for g in range(4)]
-
-    for g, value in enumerate(unmerge_half(1)):
-        gf[1, g] = value
-    b_a = net.send(gf.at[1, pl.ds(1, 2)], g1.at[0, pl.ds(2, 2)], (i, right))
-    b_b = net.send(gf.at[1, pl.ds(0, 1)], g1.at[0, pl.ds(1, 1)], (i, right))
-    b_c = net.send(gf.at[1, pl.ds(3, 1)], g1.at[0, pl.ds(0, 1)], (up, right))
-    parts = unmerge_half(0)
-    gf[0, 3] = parts[3]
-    b_d = net.send(gf.at[0, pl.ds(3, 1)], g1.at[1, pl.ds(0, 1)], (up, j))
-    for g in range(3):
-        g1[1, g + 1] = parts[g]
+        return dot(v["mer_t"][...], value).reshape(12, 6, 4, 512).astype(BF)
+
+    gf[:, far] = unmerge_half(1)
+    b_a = net.send(gf.at[pl.ds(3, 6), far], g1.at[pl.ds(6, 6), near], (i, right))
+    b_b = net.send(gf.at[first, far], g1.at[pl.ds(3, 3), near], (i, right))
+    b_c = net.send(gf.at[pl.ds(9, 3), far], g1.at[first, near], (up, right))
+    value = unmerge_half(0)
+    gf[pl.ds(9, 3), near] = value[9:]
+    b_d = net.send(gf.at[pl.ds(9, 3), near], g1.at[first, far], (up, j))
+    g1[later, far] = value[:9]
 
     x_m.wait_recv()
     attended = dot(v["mxo"][...], v["w2o_v"][own_rows, :]) + dot(v["mxr"][...], v["w2o_v"][far_rows, :])
-    result = (v["red"][...].astype(F32) + attended.astype(BF).astype(F32)).astype(BF)
-    slabs = dot(v["coa_t"][...], result)
-    for slab in range(24):
-        v["s2o"][slab // 12, slab // 3 % 4, slab % 3] = slabs[8 * slab : 8 * slab + 6].astype(BF)
-    o_a = net.send(v["s2o"].at[0], out2.at[:, pl.ds(3, 3)], (i, right))
-    o_b = net.send(v["s2o"].at[1], out2.at[:, pl.ds(0, 3)], (up, right))
+    result = v["red"][...].astype(F32) + attended.astype(BF).astype(F32)
+    for h in range(2):
+        v["s2o"][:, pl.ds(3 * h, 3)] = result[72 * h : 72 * h + 72].reshape(6, 3, 4, 1024).astype(BF)
+    o_a = net.send(v["s2o"].at[pl.ds(0, 3)], out2.at[pl.ds(3, 3)], (i, right))
+    o_b = net.send(v["s2o"].at[pl.ds(3, 3)], out2.at[pl.ds(0, 3)], (up, right))
 
     def section_one_back(w):
-        arrived = rows_of([g1[h, 2 * w + g] for h in range(2) for g in range(2)])
-        grad_blocks = dot(v["one"][...], arrived.astype(BF)).astype(BF)
+        grad_blocks = dot(v["one"][...], window_rows(g1, w).astype(BF)).astype(BF)
         v["dmix"][...] = dot(grad_blocks, v["w1o_v"][...], NT).astype(BF)
         attend_back(v["trip1"].at[w], v["dmix"], v["ps1"].at[w], v["dtrip"])
         grad = dot(v["dtrip"][...], v["w1i_v"][...], NT).astype(BF)
         grad = dot(v["one_t"][...], grad)
         grad = norm_back(grad, v["nrm"][w].astype(F32), v["rs1"][w, :, :1])
-        put_pieces(tg, w, grad + rows_of([g1[h, 2 * w + g] for h in range(2) for g in range(2)]))
+        tg[pl.ds(6 * w, 6)] = (grad + window_rows(g1, w)).reshape(6, 12, 4, 512).astype(BF)
 
     b_a.wait_recv()
     section_one_back(1)
-    t_a = net.send(tg.at[1, pl.ds(2, 1)], outg.at[0, pl.ds(3, 1)], (i, right))
-    t_b = net.send(tg.at[1, pl.ds(3, 1)], outg.at[0, pl.ds(0, 1)], (up, right))
-    t_c = net.send(tg.at[0, pl.ds(3, 1)], outg.at[1, pl.ds(0, 1)], (up, j))
-    keep_a = net.local(tg.at[0, pl.ds(2, 1)], outg.at[1, pl.ds(3, 1)])
+    t_a = net.send(tg.at[pl.ds(6, 3), far], outg.at[pl.ds(9, 3), near], (i, right))
+    t_b = net.send(tg.at[pl.ds(9, 3), far], outg.at[first, near], (up, right))
+    t_c = net.send(tg.at[pl.ds(9, 3), near], outg.at[first, far], (up, j))
+    keep_a = net.local(tg.at[pl.ds(6, 3), near], outg.at[pl.ds(9, 3), far])
     b_b.wait_recv()
     b_c.wait_recv()
     b_d.wait_recv()
     section_one_back(0)
-    t_d = net.send(tg.at[1, pl.ds(0, 2)], outg.at[0, pl.ds(1, 2)], (i, right))
-    keep_b = net.local(tg.at[0, pl.ds(0, 2)], outg.at[1, pl.ds(1, 2)])
+    t_d = net.send(tg.at[pl.ds(0, 6), far], outg.at[pl.ds(3, 6), near], (i, right))
+    keep_b = net.local(tg.at[pl.ds(0, 6), near], outg.at[pl.ds(3, 6), far])
     for copy in (o_a, o_b, t_a, t_b, t_c, t_d):
         copy.wait_recv()
     keep_a.wait()
@@ -589,7 +545,7 @@
     anywhere = pl.BlockSpec(memory_space=pl.ANY)
     out2, outg = pl.pallas_call(
         functools.partial(body, lats, lons),
-        out_shape=(jax.ShapeDtypeStruct((4, 6, 6, 1024), BF), jax.ShapeDtypeStruct((2, 4, 72, 512), BF)),
+        out_shape=(jax.ShapeDtypeStruct((6, 6, 4, 1024), BF), jax.ShapeDtypeStruct((12, 12, 4, 512), BF)),
         in_specs=[anywhere] * N_IN,
         out_specs=(anywhere, anywhere),
         scratch_shapes=[pltpu.VMEM(shape, kind) for shape, kind in shapes.values()]
@@ -598,9 +554,8 @@
             collective_id=0, has_side_effects=True, vmem_limit_bytes=56 * 2**20
         ),
         name="swin",
-    )(tokens, cotangent, *weights, *constants)
-    grad = outg.reshape(2, 4, 4, 3, 6, 512).transpose(2, 1, 3, 0, 4, 5).reshape(4, 12, 12, 512)
-    return out2, grad
+    )(tokens.transpose(1, 2, 0, 3), cotangent.transpose(1, 2, 0, 3), *weights, *constants)
+    return out2.transpose(2, 0, 1, 3), outg.transpose(2, 0, 1, 3)
 
 
 def solution(mesh):

time: 80.1 us -> 68.4 us (0.85)
  Pallas kernels: 70.8 us -> 63.7 us
  local copies, waits for them, and re-layouts: 8.34 us -> 3.91 us
    pallas_call x1, Pallas kernels: 70.8 us -> 63.7 us  [local(): pl.pallas_call(functools.partial(body, lats, lons), out_shape=(jax.ShapeD...]
    unnamed x3 -> x2, local copies, waits for them, and re-layouts: 5.86 us -> 3.91 us
    pallas_call x1 -> x0, local copies, waits for them, and re-layouts: 1.37 us -> none  [local(): pl.pallas_call(functools.partial(body, lats, lons), out_shape=(jax.ShapeD...]
    transpose x1 -> x0, local copies, waits for them, and re-layouts: 1.12 us -> none  [local(): outg.reshape(2, 4, 4, 3, 6, 512).transpose(2, 1, 3, 0, 4, 5)]
where the time goes in v2:
time: 68.4 us; the launch traced here: 68.2 us
  Pallas kernels  63.7 us (93%)
  local copies, waits for them, and re-layouts  3.91 us (6%)
    pallas_call x1, Pallas kernels, local(): pl.pallas_call(functools.partial(body, lats, lons), out_shape=(jax.ShapeD...  63.7 us
    unnamed x2, local copies, waits for them, and re-layouts  3.91 us

profile of v2, /device:TPU:2, one launch (start us, length us, event | category | flops | bytes accessed | tf_op | source)
XLA Modules:
  0.0 68.2 jit_solution(13427543783081279147)
XLA Ops:
  0.6 63.7 %swin.1 = (bf16[6,6,4,1024]{3,2,1,0:T(4,128)(2,1)}, bf16[12,12,4,512]{3,2,1,0:T(4,128)(2,1)}) custom-call(bf16[12,12,4,512]{3,2,1,0:T(4,128)(2,1)} %bitcast.4, bf16[6,6,4,1024]{3,2,1,0:T(4,128)(2,1)} %bitcast.6, bf16[512,1536]{1,0:T(8,128)(2,1)} %refs_2_.1, bf16[512,512]{1,0:T(8,128)(2,1)} %refs_3_.1, bf16[128,1024]{1,0:T(8,128)(2,1)} %refs_4_.1, ...), custom_call_target="tpu_custom_call" | custom-call | tf_op jit(solution)/shard_map/swin/pallas_call | solution.py:546
  64.3 1.8 %copy.17 = bf16[4,6,6,1024]{3,0,2,1:T(4,128)(2,1)} copy(bf16[4,6,6,1024]{3,0,2,1:T(4,128)(2,1)} %bitcast.7) | data formatting | bytes 589824
  66.1 2.1 %copy.18 = bf16[4,12,12,512]{3,0,2,1:T(4,128)(2,1)} copy(bf16[4,12,12,512]{3,0,2,1:T(4,128)(2,1)} %bitcast.5) | data formatting | bytes 1179648

commit v3 on v2

--- a/solution.py
+++ b/solution.py
@@ -539,6 +539,20 @@
         copy.wait_send()
 
 
+def hand_over(in2, ing, out2, outg, held2, heldg, in_sems, out_sems):
+    ways = [(a.at[pl.ds(3 * k, 3)], b.at[pl.ds(3 * k, 3)], c.at[pl.ds(3 * k, 3)])
+            for a, b, c, parts in ((ing, heldg, outg, 4), (in2, held2, out2, 2)) for k in range(parts)]
+    loads = [pltpu.make_async_copy(a, b, in_sems.at[n]) for n, (a, b, _) in enumerate(ways)]
+    stores = [pltpu.make_async_copy(b, c, out_sems.at[n]) for n, (_, b, c) in enumerate(ways)]
+    for load in loads:
+        load.start()
+    for load, store in zip(loads, stores):
+        load.wait()
+        store.start()
+    for store in stores:
+        store.wait()
+
+
 def local(tokens, cotangent, *weights, lats, lons):
     shapes = dict(SCRATCH, wmv=((lons, 2048 // lons, 1024), BF))
     constants = [jnp.asarray(a) for a in orders()]
@@ -555,6 +569,20 @@
         ),
         name="swin",
     )(tokens.transpose(1, 2, 0, 3), cotangent.transpose(1, 2, 0, 3), *weights, *constants)
+    out2, outg = pl.pallas_call(
+        hand_over,
+        out_shape=(jax.ShapeDtypeStruct((6, 6, 4, 1024), BF), jax.ShapeDtypeStruct((12, 12, 4, 512), BF)),
+        in_specs=[anywhere] * 2,
+        out_specs=(anywhere, anywhere),
+        scratch_shapes=[
+            pltpu.VMEM((6, 6, 4, 1024), BF),
+            pltpu.VMEM((12, 12, 4, 512), BF),
+            pltpu.SemaphoreType.DMA((6,)),
+            pltpu.SemaphoreType.DMA((6,)),
+        ],
+        compiler_params=pltpu.CompilerParams(vmem_limit_bytes=56 * 2**20),
+        name="hand",
+    )(out2, outg)
     return out2.transpose(2, 0, 1, 3), outg.transpose(2, 0, 1, 3)
 
 

time: 68.4 us -> 66.6 us (0.974)
  local copies, waits for them, and re-layouts: 3.91 us -> 0 us
  Pallas kernels: 63.7 us -> 65.7 us
    unnamed x2 -> x0, local copies, waits for them, and re-layouts: 3.91 us -> none
    pallas_call x0 -> x1, Pallas kernels: none -> 2.02 us  [local(): pl.pallas_call(hand_over, out_shape=(jax.ShapeDtypeStruct((6, 6, 4, 1024)...]
where the time goes in v3:
time: 66.6 us; the launch traced here: 66.5 us
  Pallas kernels  65.7 us (99%)
  between operations  0.8 us (1%)
    pallas_call x1, Pallas kernels, local(): pl.pallas_call(functools.partial(body, lats, lons), out_shape=(jax.ShapeD...  63.7 us
    pallas_call x1, Pallas kernels, local(): pl.pallas_call(hand_over, out_shape=(jax.ShapeDtypeStruct((6, 6, 4, 1024)...  2.02 us

profile of v3, /device:TPU:2, one launch (start us, length us, event | category | flops | bytes accessed | tf_op | source)
XLA Modules:
  0.0 66.5 jit_solution(11064767447315669476)
XLA Ops:
  0.6 63.7 %swin.1 = (bf16[6,6,4,1024]{3,2,1,0:T(4,128)(2,1)}, bf16[12,12,4,512]{3,2,1,0:T(4,128)(2,1)}) custom-call(bf16[12,12,4,512]{3,2,1,0:T(4,128)(2,1)} %bitcast.4, bf16[6,6,4,1024]{3,2,1,0:T(4,128)(2,1)} %bitcast.5, bf16[512,1536]{1,0:T(8,128)(2,1)} %refs_2_.1, bf16[512,512]{1,0:T(8,128)(2,1)} %refs_3_.1, bf16[128,1024]{1,0:T(8,128)(2,1)} %refs_4_.1, ...), custom_call_target="tpu_custom_call" | custom-call | tf_op jit(solution)/shard_map/swin/pallas_call | solution.py:560
  64.3 2.0 %hand.1 = (bf16[6,6,4,1024]{3,2,1,0:T(4,128)(2,1)}, bf16[12,12,4,512]{3,2,1,0:T(4,128)(2,1)}) custom-call(bf16[6,6,4,1024]{3,2,1,0:T(4,128)(2,1)} %get-tuple-element.6.in2, bf16[12,12,4,512]{3,2,1,0:T(4,128)(2,1)} %get-tuple-element.7.ing), custom_call_target="tpu_custom_call" | custom-call | tf_op jit(solution)/shard_map/hand/pallas_call | solution.py:572

commit v4 on v3

--- a/solution.py
+++ b/solution.py
@@ -461,11 +461,17 @@
     v["dmix2"][...] = dot(grad_blocks, v["w2o_v"][own_rows, :], NT).astype(BF)
     for copy in in_w2i + in_late:
         copy.wait()
+
+    def project_two(m):
+        for n in range(0, 1536, 256):
+            part = dot(v["nt"][m], v["w2i_v"][:, pl.ds(n, 256)]).astype(BF)
+            v["dtrip"][pl.ds(144 * m, 144), pl.ds(n, 256)] = part
+
+    project_two(0)
     n_m.wait_recv()
-
-    blocks = dot(v["two"][...], v["nt"][...].reshape(288, 1024)).astype(BF)
+    project_two(1)
     for n in range(0, 1536, 256):
-        v["trip2"][:, pl.ds(n, 256)] = dot(blocks, v["w2i_v"][:, pl.ds(n, 256)]).astype(BF)
+        v["trip2"][:, pl.ds(n, 256)] = dot(v["two"][...], v["dtrip"][:, pl.ds(n, 256)]).astype(BF)
     attend(v["trip2"], v["mk"].at[1], v["mix2"], v["ps2"])
     mixed = dot(v["two_t"][...], v["mix2"][...]).astype(BF)
     v["mxo"][...] = mixed[:144]

time: 66.6 us -> 66.7 us (level)
  no operation moved by 1% of the time
where the time goes in v4:
time: 66.7 us; the launch traced here: 66.6 us
  Pallas kernels  65.8 us (99%)
  between operations  0.8 us (1%)
    pallas_call x1, Pallas kernels, local(): pl.pallas_call(functools.partial(body, lats, lons), out_shape=(jax.ShapeD...  63.8 us
    pallas_call x1, Pallas kernels, local(): pl.pallas_call(hand_over, out_shape=(jax.ShapeDtypeStruct((6, 6, 4, 1024)...  2.02 us

profile of v4, /device:TPU:2, one launch (start us, length us, event | category | flops | bytes accessed | tf_op | source)
XLA Modules:
  0.0 66.6 jit_solution(5280081652884920738)
XLA Ops:
  0.6 63.8 %swin.1 = (bf16[6,6,4,1024]{3,2,1,0:T(4,128)(2,1)}, bf16[12,12,4,512]{3,2,1,0:T(4,128)(2,1)}) custom-call(bf16[12,12,4,512]{3,2,1,0:T(4,128)(2,1)} %bitcast.4, bf16[6,6,4,1024]{3,2,1,0:T(4,128)(2,1)} %bitcast.5, bf16[512,1536]{1,0:T(8,128)(2,1)} %refs_2_.1, bf16[512,512]{1,0:T(8,128)(2,1)} %refs_3_.1, bf16[128,1024]{1,0:T(8,128)(2,1)} %refs_4_.1, ...), custom_call_target="tpu_custom_call" | custom-call | tf_op jit(solution)/shard_map/swin/pallas_call | solution.py:566
  64.5 2.0 %hand.1 = (bf16[6,6,4,1024]{3,2,1,0:T(4,128)(2,1)}, bf16[12,12,4,512]{3,2,1,0:T(4,128)(2,1)}) custom-call(bf16[6,6,4,1024]{3,2,1,0:T(4,128)(2,1)} %get-tuple-element.6.in2, bf16[12,12,4,512]{3,2,1,0:T(4,128)(2,1)} %get-tuple-element.7.ing), custom_call_target="tpu_custom_call" | custom-call | tf_op jit(solution)/shard_map/hand/pallas_call | solution.py:578
